TPU v7x, 256 devices: a whole 4x4x8 slice. The times are simulated.
256 devices in a mesh: dp: 32 (over z, x), fsdp: 8 (over y, core).
Axes of the slice: x: 4, y: 4, z: 8, core: 2. Of those that a mesh axis runs over, the one named last changes fastest.
Arguments:
- patches: bfloat16 [131072, 1152], P(('dp', 'fsdp')), may hold values from -6 to 6
- layer_norm_gain: float32 [1152], replicated, may hold values from 0.25 to 1.75
- layer_norm_bias: float32 [1152], replicated, may hold values from -3 to 3
- w_qkv: bfloat16 [1152, 1728], P('fsdp'), may hold values from -0.1875 to 0.1875
- qkv_bias: float32 [1728], replicated, may hold values from -3 to 3
- out_grad: bfloat16 [131072, 576], P(('dp', 'fsdp')), may hold values from -6 to 6
- lengths: int32 [512], P(('dp', 'fsdp')), may hold values from 1 to 256, as said below
- target: int32 [512], P(('dp', 'fsdp')), may hold values from 0 to 31, as said below
Outputs:
- attn_out: bfloat16 [131072, 576], P(('dp', 'fsdp'))
- patch_gradient: bfloat16 [131072, 1152], P(('dp', 'fsdp'))
- weight_grad: float32 [1152, 1728], P('fsdp')
- gain_gradient: float32 [1152], replicated
- bias_grad: float32 [1152], replicated
- qkv_bias_grad: float32 [1728], replicated
Inputs may be any that keep to these rules, and one draw needn't show every extreme that they name: `target`: for each fsdp index and slot position s there is a number m, 0 <= m < 32, such that the slot of position s on dp index d goes to dp index d XOR m. `lengths`: every device holds a slot of 256 patches.
All inputs are finite; a program needn't handle non-finite values.
Results may differ from a plain program's by a relative error of at most 0.025.
Values may be sent and summed in bfloat16 or wider, within the bound.
A program may use at most 128 MiB of HBM per device.

v0:
```python
import jax
import jax.numpy as jnp
from jax import lax
from jax.sharding import PartitionSpec as P

HEADS = 8
HD = 72


def swapped(value, axis, distance):
    mask = 2**distance
    pairs = [(source, source ^ mask) for source in range(lax.axis_size(axis))]
    return lax.ppermute(value, axis, pairs)


def layer_statistics(patches):
    values = patches.astype(jnp.float32)
    center = values - jnp.mean(values, axis=-1, keepdims=True)
    variance = jnp.mean(center * center, axis=-1, keepdims=True)
    inverse_deviation = lax.rsqrt(variance + 1e-06)
    return (center * inverse_deviation, inverse_deviation)


def attend(qkv_slot, grad_slot, length):
    width = HEADS * HD
    count = qkv_slot.shape[0]
    query = qkv_slot[:, :width].reshape(count, HEADS, HD)
    keys = qkv_slot[:, width : 2 * width].reshape(count, HEADS, HD)
    values = qkv_slot[:, 2 * width :].reshape(count, HEADS, HD)
    positions = jnp.arange(count, dtype=jnp.int32)
    live = positions < length
    score_scale = 1.0 / HD**0.5
    scores = (
        jnp.einsum("qhd,khd->hqk", query, keys, preferred_element_type=jnp.float32) * score_scale
    )
    scores = jnp.where(live[None, None, :], scores, -1e30)
    top = jnp.max(scores, axis=-1, keepdims=True)
    weights = jnp.exp(scores - top) * live[None, None, :].astype(jnp.float32)
    probs = weights / jnp.sum(weights, axis=-1, keepdims=True)
    rounded = probs.astype(jnp.bfloat16)
    output = jnp.einsum("hqk,khd->qhd", rounded, values, preferred_element_type=jnp.float32)
    output = jnp.where(live[:, None, None], output, 0.0).astype(jnp.bfloat16).reshape(count, width)
    upstream = jnp.where(
        live[:, None, None], grad_slot.reshape(count, HEADS, HD), jnp.zeros((), jnp.bfloat16)
    )
    grad_values = jnp.einsum("hqk,qhd->khd", rounded, upstream, preferred_element_type=jnp.float32)
    grad_probs = jnp.einsum("qhd,khd->hqk", upstream, values, preferred_element_type=jnp.float32)
    delta = jnp.sum(grad_probs * probs, axis=-1, keepdims=True)
    grad_scores = (probs * (grad_probs - delta) * score_scale).astype(jnp.bfloat16)
    grad_query = jnp.einsum("hqk,khd->qhd", grad_scores, keys, preferred_element_type=jnp.float32)
    grad_keys = jnp.einsum("hqk,qhd->khd", grad_scores, query, preferred_element_type=jnp.float32)
    joined = jnp.concatenate(
        [
            grad_query.reshape(count, width),
            grad_keys.reshape(count, width),
            grad_values.reshape(count, width),
        ],
        axis=1,
    )
    return (output, joined.astype(jnp.bfloat16))


def flips_at(mask, bit_number):
    return (jnp.bitwise_and(jnp.right_shift(mask, bit_number), 1) == 1)[:, None, None]


def body(patches, layer_norm_gain, layer_norm_bias, w_qkv, qkv_bias, out_grad, lengths, target):
    width = HEADS * HD
    slot_total = lengths.shape[0]
    slot_rows = patches.shape[0] // slot_total
    peers = lax.axis_size("dp")
    bit_count = peers.bit_length() - 1
    myself = lax.axis_index("dp")
    all_lengths = lax.all_gather(lengths, "dp", axis=0, tiled=True).reshape(peers, slot_total)
    mask = jnp.bitwise_xor(target, myself)
    here_lengths = all_lengths[target, jnp.arange(slot_total, dtype=jnp.int32)]
    full_weight = lax.all_gather(w_qkv, "fsdp", axis=0, tiled=True)
    centered_scaled_input, inverse_deviation = layer_statistics(patches)
    normalized_input = (centered_scaled_input * layer_norm_gain + layer_norm_bias).astype(
        jnp.bfloat16
    )
    grad_here = out_grad.reshape(slot_total, slot_rows, width)
    attend_all = jax.vmap(attend)
    qkv = (
        jnp.dot(normalized_input, full_weight, preferred_element_type=jnp.float32) + qkv_bias
    ).astype(jnp.bfloat16)
    moving = qkv.reshape(slot_total, slot_rows, 3 * width)
    for bit_number in range(bit_count):
        partner = swapped(moving, "dp", bit_number)
        moving = jnp.where(flips_at(mask, bit_number), partner, moving)
    outputs, grads = attend_all(moving, grad_here, here_lengths)
    for bit_number in range(bit_count):
        partner = swapped(grads, "dp", bit_number)
        grads = jnp.where(flips_at(mask, bit_number), partner, grads)
    dqkv = grads.reshape(-1, 3 * width)
    partial_weight = jnp.dot(normalized_input.T, dqkv, preferred_element_type=jnp.float32)
    partial_qbias = jnp.sum(dqkv.astype(jnp.float32), axis=0)
    normalized_gradient = jnp.dot(dqkv, full_weight.T, preferred_element_type=jnp.float32).astype(
        jnp.bfloat16
    )
    attn_out = outputs.reshape(-1, width)
    norm_value_gradient = normalized_gradient.astype(jnp.float32)
    partial_gain_gradient = jnp.sum(norm_value_gradient * centered_scaled_input, axis=0)
    partial_bias = jnp.sum(norm_value_gradient, axis=0)
    scaled_input = norm_value_gradient * layer_norm_gain
    patch_gradient = inverse_deviation * (
        scaled_input
        - jnp.mean(scaled_input, axis=-1, keepdims=True)
        - centered_scaled_input
        * jnp.mean(scaled_input * centered_scaled_input, axis=-1, keepdims=True)
    )
    gain_gradient, bias_grad, qkv_bias_grad = lax.psum(
        (partial_gain_gradient, partial_bias, partial_qbias), ("dp", "fsdp")
    )
    owned = lax.psum_scatter(
        partial_weight.astype(jnp.bfloat16), "fsdp", scatter_dimension=0, tiled=True
    )
    weight_grad = lax.psum(owned, "dp").astype(jnp.float32)
    return (
        attn_out,
        patch_gradient.astype(jnp.bfloat16),
        weight_grad,
        gain_gradient,
        bias_grad,
        qkv_bias_grad,
    )


def solution(mesh):
    return jax.shard_map(
        body,
        mesh=mesh,
        in_specs=(
            P(("dp", "fsdp"), None),
            P(),
            P(),
            P("fsdp", None),
            P(),
            P(("dp", "fsdp"), None),
            P(("dp", "fsdp")),
            P(("dp", "fsdp")),
        ),
        out_specs=(
            P(("dp", "fsdp"), None),
            P(("dp", "fsdp"), None),
            P("fsdp", None),
            P(),
            P(),
            P(),
        ),
        check_vma=False,
    )
```

profile of v0, /device:TPU:8, one launch (start us, length us, event | category | flops | bytes accessed | tf_op | source)
XLA Modules:
  0.0 930.5 jit_solution(5931524232839153605)
XLA Ops:
  8.0 1.5 convert_reduce_fusion.2
  10.0 36.2 %all-gather.2.cloned.1.call-done = bf16[1152,1728]{1,0:T(8,128)(2,1)} async-done(((bf16[144,1728]{1,0:T(8,128)(2,1)}), bf16[1152,1728]{1,0:T(8,128)(2,1)}) %all-gather.2.cloned.1.call-update) | async-done | bytes 3981328 | tf_op jit(solution)/shard_map/all_gather | solution.py:77
  46.2 6.1 add_convert_fusion
  52.3 3.9 reshape.128
  56.3 1.6 collective-permute-start
  58.4 38.9 %collective-permute-done = bf16[2,256,1728]{1,0,2:T(2,128)(2,1)} collective-permute-done((bf16[2,256,1728]{1,0,2:T(2,128)(2,1)S(1)}, bf16[2,256,1728]{1,0,2:T(2,128)(2,1)}, u32[]{:S(2)}, u32[]{:S(2)}) %collective-permute-start) | collective-permute-done | bytes 1769504 | tf_op jit(solution)/shard_map/ppermute | solution.py:13
  97.2 3.5 broadcast_select_fusion.1
  100.8 3.1 collective-permute-start.1
  103.8 38.5 %collective-permute-done.1 = bf16[2,256,1728]{1,0,2:T(2,128)(2,1)S(1)} collective-permute-done((bf16[2,256,1728]{1,0,2:T(2,128)(2,1)S(1)}, bf16[2,256,1728]{1,0,2:T(2,128)(2,1)S(1)}, u32[]{:S(2)}, u32[]{:S(2)}) %collective-permute-start.1) | collective-permute-done | bytes 1769504 | tf_op jit(solution)/shard_map/ppermute | solution.py:13
  142.3 2.1 broadcast_select_fusion.3
  144.4 1.6 collective-permute-start.2
  146.1 37.5 %collective-permute-done.2 = bf16[2,256,1728]{1,0,2:T(2,128)(2,1)S(1)} collective-permute-done((bf16[2,256,1728]{1,0,2:T(2,128)(2,1)S(1)}, bf16[2,256,1728]{1,0,2:T(2,128)(2,1)S(1)}, u32[]{:S(2)}, u32[]{:S(2)}) %collective-permute-start.2) | collective-permute-done | bytes 1769504 | tf_op jit(solution)/shard_map/ppermute | solution.py:13
  183.5 2.1 broadcast_select_fusion.5
  185.6 2.6 collective-permute-start.3
  188.3 74.4 %collective-permute-done.3 = bf16[2,256,1728]{1,0,2:T(2,128)(2,1)S(1)} collective-permute-done((bf16[2,256,1728]{1,0,2:T(2,128)(2,1)S(1)}, bf16[2,256,1728]{1,0,2:T(2,128)(2,1)S(1)}, u32[]{:S(2)}, u32[]{:S(2)}) %collective-permute-start.3) | collective-permute-done | bytes 1769504 | tf_op jit(solution)/shard_map/ppermute | solution.py:13
  262.6 2.1 broadcast_select_fusion.7
  264.8 5.8 collective-permute-start.4
  272.1 81.8 %all-reduce = s32[64]{0:T(128)S(1)} all-reduce(s32[64]{0:T(128)S(1)} %dynamic-update-slice), channel_id=1, replica_groups=mesh['dp'=32,'fsdp'=8] {'dp'}, use_global_device_ids=true, to_apply=%add | all-reduce | flops 64 | bytes 512
  354.0 1.9 reshape_reshape.3
  355.9 1.2 fusion.51
  357.1 1.3 gather_fusion
  359.1 3.6 broadcast_select_fusion.9
  362.6 1.2 fusion.63
  365.8 2.7 fusion.42
  368.5 4.5 fusion.64
  373.0 8.1 fusion.33
  381.0 8.0 fusion.36
  389.1 3.1 convolution_convert_fusion.2
  394.1 1.7 collective-permute-start.5
  395.8 37.2 %collective-permute-done.5 = bf16[2,256,1728]{1,0,2:T(2,128)(2,1)S(1)} collective-permute-done((bf16[2,256,1728]{1,0,2:T(2,128)(2,1)S(1)}, bf16[2,256,1728]{1,0,2:T(2,128)(2,1)S(1)}, u32[]{:S(2)}, u32[]{:S(2)}) %collective-permute-start.5) | collective-permute-done | bytes 1769504 | tf_op jit(solution)/shard_map/ppermute | solution.py:13
  433.0 2.1 broadcast_select_fusion
  435.1 3.1 collective-permute-start.6
  438.2 36.3 %collective-permute-done.6 = bf16[2,256,1728]{1,0,2:T(2,128)(2,1)S(1)} collective-permute-done((bf16[2,256,1728]{1,0,2:T(2,128)(2,1)S(1)}, bf16[2,256,1728]{1,0,2:T(2,128)(2,1)S(1)}, u32[]{:S(2)}, u32[]{:S(2)}) %collective-permute-start.6) | collective-permute-done | bytes 1769504 | tf_op jit(solution)/shard_map/ppermute | solution.py:13
  474.5 2.1 broadcast_select_fusion.2
  476.7 36.8 %collective-permute-done.7 = bf16[2,256,1728]{1,0,2:T(2,128)(2,1)S(1)} collective-permute-done((bf16[2,256,1728]{1,0,2:T(2,128)(2,1)S(1)}, bf16[2,256,1728]{1,0,2:T(2,128)(2,1)S(1)}, u32[]{:S(2)}, u32[]{:S(2)}) %collective-permute-start.7) | collective-permute-done | bytes 1769504 | tf_op jit(solution)/shard_map/ppermute | solution.py:13
  513.5 2.1 broadcast_select_fusion.4
  515.8 74.7 %collective-permute-done.8 = bf16[2,256,1728]{1,0,2:T(2,128)(2,1)S(1)} collective-permute-done((bf16[2,256,1728]{1,0,2:T(2,128)(2,1)S(1)}, bf16[2,256,1728]{1,0,2:T(2,128)(2,1)S(1)}, u32[]{:S(2)}, u32[]{:S(2)}) %collective-permute-start.8) | collective-permute-done | bytes 1769504 | tf_op jit(solution)/shard_map/ppermute | solution.py:13
  590.5 2.1 broadcast_select_fusion.6
  592.6 2.4 collective-permute-start.9
  595.0 79.0 %collective-permute-done.9 = bf16[2,256,1728]{1,0,2:T(2,128)(2,1)S(1)} collective-permute-done((bf16[2,256,1728]{1,0,2:T(2,128)(2,1)S(1)}, bf16[2,256,1728]{1,0,2:T(2,128)(2,1)S(1)}, u32[]{:S(2)}, u32[]{:S(2)}) %collective-permute-start.9) | collective-permute-done | bytes 1769504 | tf_op jit(solution)/shard_map/ppermute | solution.py:13
  674.0 13.4 %convert_reduce_fusion = (f32[1728]{0:T(1024)S(1)}, bf16[2,256,1728]{1,0,2:T(2,128)(2,1)S(1)}) fusion(bf16[2,256,1728]{1,0,2:T(2,128)(2,1)S(1)} %collective-permute-done.9, bf16[2,256,1728]{1,0,2:T(2,128)(2,1)S(1)} %broadcast_select_fusion.6, pred[2]{0:T(512)(128)(4,1)S(1)} %copy-done.20), kind=kLoop, calls=%fused_computation.9 | loop fusion | flops 2652480 | bytes 5315330 | tf_op jit(solution)/shard_map/reduce_sum | solution.py:97
  688.1 4.7 convolution_convert_fusion
  693.1 2.8 fusion.39
  697.5 4.2 fusion.26
  701.7 75.0 %all-reduce.1 = (f32[1152]{0:T(1024)}, f32[1152]{0:T(1024)}, f32[1728]{0:T(1024)}) all-reduce(f32[1152]{0:T(1024)S(1)} %get-tuple-element.6, f32[1152]{0:T(1024)S(1)} %get-tuple-element.9, f32[1728]{0:T(1024)S(1)} %get-tuple-element.13), channel_id=1, replica_groups=mesh['dp'=32,'fsdp'=8] {'dp','fsdp'}, use_global_device_ids=true, to_apply=%region_10.11 | all-reduce | flops 4032 | bytes 32256 | tf_op jit(solution)/shard_map/psum | solution.py:112
  776.8 3.1 fusion.23
  779.8 141.8 %all-reduce.4.cloned.1.call-done = bf16[144,1728]{1,0:T(8,128)(2,1)} async-done(((bf16[144,1728]{1,0:T(8,128)(2,1)}), bf16[144,1728]{1,0:T(8,128)(2,1)}) %all-reduce.4.cloned.1.call-update) | async-done | bytes 497680 | tf_op jit(solution)/shard_map/psum | solution.py:118
  921.6 2.1 convert_element_type.61
  (88 shorter events, 10.0 us)
Async XLA Ops:
  7.2 2.3 copy-start
  7.2 39.0 %copy-start.9 = (f32[1152]{0:T(1024)S(1)}, f32[1152]{0:T(1024)}, u32[]{:S(2)}) copy-start(f32[1152]{0:T(1024)} %param.9) | copy-start | bytes 13828
  7.2 39.0 %copy-start.25 = (f32[1152]{0:T(1024)S(1)}, f32[1152]{0:T(1024)}, u32[]{:S(2)}) copy-start(f32[1152]{0:T(1024)} %param.10) | copy-start | bytes 13828
  7.2 39.0 %copy-start.24 = (f32[1728]{0:T(1024)S(1)}, f32[1728]{0:T(1024)}, u32[]{:S(2)}) copy-start(f32[1728]{0:T(1024)} %param.12) | copy-start | bytes 20740
  7.2 39.0 %all-gather.2.cloned.1.call-start = ((), (), s32[]{:S(2)}) async-start(), calls=%async_computation.1 | async-start | bytes 4644864 | tf_op jit(solution)/shard_map/all_gather | solution.py:77
  7.9 768.8 %reduce-scatter.2.cloned.1.call-start = ((), (), s32[]{:S(2)}) async-start(), calls=%async_computation.2 | async-start | bytes 4644864 | tf_op jit(solution)/shard_map/reduce_scatter | solution.py:115
  9.5 36.7 %copy-start.5 = (f32[512]{0:T(512)}, f32[512]{0:T(512)S(1)}, u32[]{:S(2)}) copy-start(f32[512]{0:T(512)S(1)} %broadcast_multiply_fusion.2) | copy-start | bytes 6148
  10.0 36.2 %copy-start.7 = (f32[512]{0:T(512)}, f32[512]{0:T(512)S(1)}, u32[]{:S(2)}) copy-start(f32[512]{0:T(512)S(1)} %add_rsqrt_fusion) | copy-start | bytes 6148
  52.3 5.5 copy-start.22
  56.3 40.9 %collective-permute-start = (bf16[2,256,1728]{1,0,2:T(2,128)(2,1)S(1)}, bf16[2,256,1728]{1,0,2:T(2,128)(2,1)}, u32[]{:S(2)}, u32[]{:S(2)}) collective-permute-start(bf16[2,256,1728]{1,0,2:T(2,128)(2,1)S(1)} %reshape.128), channel_id=1, source_target_pairs={{0,8},{8,0},{16,24},{24,16},{32,40},{40,32},{48,56},{56,48},{64,72... | collective-permute-start | bytes 5308424 | tf_op jit(solution)/shard_map/ppermute | solution.py:13
  58.3 42.4 %copy-start.18 = (pred[2]{0:T(512)(128)(4,1)}, pred[2]{0:T(512)(128)(4,1)S(1)}, u32[]{:S(2)}) copy-start(pred[2]{0:T(512)(128)(4,1)S(1)} %get-tuple-element.25) | copy-start | bytes 10
  58.3 84.0 %copy-start.16 = (pred[2]{0:T(512)(128)(4,1)}, pred[2]{0:T(512)(128)(4,1)S(1)}, u32[]{:S(2)}) copy-start(pred[2]{0:T(512)(128)(4,1)S(1)} %get-tuple-element.23) | copy-start | bytes 10
  58.3 125.2 %copy-start.14 = (pred[2]{0:T(512)(128)(4,1)}, pred[2]{0:T(512)(128)(4,1)S(1)}, u32[]{:S(2)}) copy-start(pred[2]{0:T(512)(128)(4,1)S(1)} %get-tuple-element.24) | copy-start | bytes 10
  58.3 204.3 %copy-start.12 = (pred[2]{0:T(512)(128)(4,1)}, pred[2]{0:T(512)(128)(4,1)S(1)}, u32[]{:S(2)}) copy-start(pred[2]{0:T(512)(128)(4,1)S(1)} %get-tuple-element.22) | copy-start | bytes 10
  100.8 41.5 %collective-permute-start.1 = (bf16[2,256,1728]{1,0,2:T(2,128)(2,1)S(1)}, bf16[2,256,1728]{1,0,2:T(2,128)(2,1)S(1)}, u32[]{:S(2)}, u32[]{:S(2)}) collective-permute-start(bf16[2,256,1728]{1,0,2:T(2,128)(2,1)S(1)} %broadcast_select_fusion.1), channel_id=1, source_target_pairs={{0,16},{8,24},{16,0},{24,8},{32,48},{40,56},{48,32},{56,40},{64,80... | collective-permute-start | bytes 5308424 | tf_op jit(solution)/shard_map/ppermute | solution.py:13
  144.4 39.1 %collective-permute-start.2 = (bf16[2,256,1728]{1,0,2:T(2,128)(2,1)S(1)}, bf16[2,256,1728]{1,0,2:T(2,128)(2,1)S(1)}, u32[]{:S(2)}, u32[]{:S(2)}) collective-permute-start(bf16[2,256,1728]{1,0,2:T(2,128)(2,1)S(1)} %broadcast_select_fusion.3), channel_id=1, source_target_pairs={{0,32},{8,40},{16,48},{24,56},{32,0},{40,8},{48,16},{56,24},{64,96... | collective-permute-start | bytes 5308424 | tf_op jit(solution)/shard_map/ppermute | solution.py:13
  185.6 77.0 %collective-permute-start.3 = (bf16[2,256,1728]{1,0,2:T(2,128)(2,1)S(1)}, bf16[2,256,1728]{1,0,2:T(2,128)(2,1)S(1)}, u32[]{:S(2)}, u32[]{:S(2)}) collective-permute-start(bf16[2,256,1728]{1,0,2:T(2,128)(2,1)S(1)} %broadcast_select_fusion.5), channel_id=1, source_target_pairs={{0,64},{8,72},{16,80},{24,88},{32,96},{40,104},{48,112},{56,120},{... | collective-permute-start | bytes 5308424 | tf_op jit(solution)/shard_map/ppermute | solution.py:13
  262.6 8.0 copy-start.28
  262.6 9.2 copy-start.27
  264.8 94.3 %collective-permute-start.4 = (bf16[2,256,1728]{1,0,2:T(2,128)(2,1)S(1)}, bf16[2,256,1728]{1,0,2:T(2,128)(2,1)}, u32[]{:S(2)}, u32[]{:S(2)}) collective-permute-start(bf16[2,256,1728]{1,0,2:T(2,128)(2,1)S(1)} %broadcast_select_fusion.7), channel_id=1, source_target_pairs={{0,128},{8,136},{16,144},{24,152},{32,160},{40,168},{48,176},{56,1... | collective-permute-start | bytes 5308424 | tf_op jit(solution)/shard_map/ppermute | solution.py:13
  359.1 30.0 %copy-start.21 = (pred[2,256]{1,0:T(4,128)(4,1)}, pred[2,256]{1,0:T(4,128)(4,1)S(1)}, u32[]{:S(2)}) copy-start(pred[2,256]{1,0:T(4,128)(4,1)S(1)} %get-tuple-element.21) | copy-start | bytes 1540
  365.7 2.7 copy-start.1
  365.7 2.7 copy-start.2
  389.1 3.1 copy-start.3
  389.1 3.7 copy-start.4
  392.1 40.9 %copy-start.19 = (pred[2]{0:T(512)(128)(4,1)S(1)}, pred[2]{0:T(512)(128)(4,1)}, u32[]{:S(2)}) copy-start(pred[2]{0:T(512)(128)(4,1)} %copy-done.18) | copy-start | bytes 10
  394.1 80.4 %copy-start.17 = (pred[2]{0:T(512)(128)(4,1)S(1)}, pred[2]{0:T(512)(128)(4,1)}, u32[]{:S(2)}) copy-start(pred[2]{0:T(512)(128)(4,1)} %copy-done.16) | copy-start | bytes 10
  394.1 38.9 %collective-permute-start.5 = (bf16[2,256,1728]{1,0,2:T(2,128)(2,1)S(1)}, bf16[2,256,1728]{1,0,2:T(2,128)(2,1)S(1)}, u32[]{:S(2)}, u32[]{:S(2)}) collective-permute-start(bf16[2,256,1728]{1,0,2:T(2,128)(2,1)S(1)} %copy_dynamic-update-slice_fusion), channel_id=1, source_target_pairs={{0,8},{8,0},{16,24},{24,16},{32,40},{40,32},{48,56},{56,48},{64,72... | collective-permute-start | bytes 5308424 | tf_op jit(solution)/shard_map/ppermute | solution.py:13
  435.1 78.4 %copy-start.15 = (pred[2]{0:T(512)(128)(4,1)S(1)}, pred[2]{0:T(512)(128)(4,1)}, u32[]{:S(2)}) copy-start(pred[2]{0:T(512)(128)(4,1)} %copy-done.14) | copy-start | bytes 10
  435.1 39.3 %collective-permute-start.6 = (bf16[2,256,1728]{1,0,2:T(2,128)(2,1)S(1)}, bf16[2,256,1728]{1,0,2:T(2,128)(2,1)S(1)}, u32[]{:S(2)}, u32[]{:S(2)}) collective-permute-start(bf16[2,256,1728]{1,0,2:T(2,128)(2,1)S(1)} %broadcast_select_fusion), channel_id=1, source_target_pairs={{0,16},{8,24},{16,0},{24,8},{32,48},{40,56},{48,32},{56,40},{64,80... | collective-permute-start | bytes 5308424 | tf_op jit(solution)/shard_map/ppermute | solution.py:13
  476.6 113.9 %copy-start.13 = (pred[2]{0:T(512)(128)(4,1)S(1)}, pred[2]{0:T(512)(128)(4,1)}, u32[]{:S(2)}) copy-start(pred[2]{0:T(512)(128)(4,1)} %copy-done.12) | copy-start | bytes 10
  476.6 36.9 %collective-permute-start.7 = (bf16[2,256,1728]{1,0,2:T(2,128)(2,1)S(1)}, bf16[2,256,1728]{1,0,2:T(2,128)(2,1)S(1)}, u32[]{:S(2)}, u32[]{:S(2)}) collective-permute-start(bf16[2,256,1728]{1,0,2:T(2,128)(2,1)S(1)} %broadcast_select_fusion.2), channel_id=1, source_target_pairs={{0,32},{8,40},{16,48},{24,56},{32,0},{40,8},{48,16},{56,24},{64,96... | collective-permute-start | bytes 5308424 | tf_op jit(solution)/shard_map/ppermute | solution.py:13
  515.7 158.3 %copy-start.20 = (pred[2]{0:T(512)(128)(4,1)S(1)}, pred[2]{0:T(512)(128)(4,1)}, u32[]{:S(2)}) copy-start(pred[2]{0:T(512)(128)(4,1)} %get-tuple-element.15) | copy-start | bytes 10
  515.7 74.8 %collective-permute-start.8 = (bf16[2,256,1728]{1,0,2:T(2,128)(2,1)S(1)}, bf16[2,256,1728]{1,0,2:T(2,128)(2,1)S(1)}, u32[]{:S(2)}, u32[]{:S(2)}) collective-permute-start(bf16[2,256,1728]{1,0,2:T(2,128)(2,1)S(1)} %broadcast_select_fusion.4), channel_id=1, source_target_pairs={{0,64},{8,72},{16,80},{24,88},{32,96},{40,104},{48,112},{56,120},{... | collective-permute-start | bytes 5308424 | tf_op jit(solution)/shard_map/ppermute | solution.py:13
  592.6 81.4 %collective-permute-start.9 = (bf16[2,256,1728]{1,0,2:T(2,128)(2,1)S(1)}, bf16[2,256,1728]{1,0,2:T(2,128)(2,1)S(1)}, u32[]{:S(2)}, u32[]{:S(2)}) collective-permute-start(bf16[2,256,1728]{1,0,2:T(2,128)(2,1)S(1)} %broadcast_select_fusion.6), channel_id=1, source_target_pairs={{0,128},{8,136},{16,144},{24,152},{32,160},{40,168},{48,176},{56,1... | collective-permute-start | bytes 5308424 | tf_op jit(solution)/shard_map/ppermute | solution.py:13
  687.4 0.7 copy-start.6
  687.4 0.7 copy-start.8
  687.4 0.7 copy-start.10
  687.4 0.7 copy-start.26
  692.8 228.8 %all-reduce.4.cloned.1.call-start = ((), (), s32[]{:S(2)}) async-start(), calls=%async_computation.3 | async-start | bytes 1032192 | tf_op jit(solution)/shard_map/psum | solution.py:118
  693.1 4.4 copy-start.23
  696.0 1.5 copy-start.11
Sparse Core Ops, SparseCore 0:
  9.9 36.2 all-gather.1
  693.0 35.5 reduce-scatter.1
  776.9 144.7 all-reduce.3
where the time goes:
time: 939 us; the launch traced here: 930 us
  waiting for transfers between devices  632 us (67%)
  blocking collectives  157 us (17%)
  other arithmetic  44.8 us (5%)
  matrix products  44.2 us (5%)
  starting transfers between devices  22.5 us (2%)
  local copies, waits for them, and re-layouts  15.4 us (2%)
  between operations  15.1 us (2%)
    ppermute x10, waiting for transfers between devices, swapped(): return lax.ppermute(value, axis, pairs)  453 us
    psum x1, waiting for transfers between devices, body(): weight_grad = lax.psum(owned, 'dp').astype(jnp.float32)  142 us
    unnamed x1, blocking collectives  81.8 us
    psum x1, blocking collectives, body(): lax.psum((partial_gain_gradient, partial_bias, partial_qbias), ('dp', 'fs...  75 us
    all_gather x1, waiting for transfers between devices, body(): full_weight = lax.all_gather(w_qkv, 'fsdp', axis=0, tiled=True)  36.2 us
    ppermute x10, starting transfers between devices, swapped(): return lax.ppermute(value, axis, pairs)  22.1 us
  transfers between devices with their start and end apart: 13, of which 11 were waited for; matrix products, arithmetic and copies ran while one was open for 2% of the time, Pallas kernels for 0%

commit v1 on v0

v1 whole, which is shorter than its diff:
```python
import jax
import jax.numpy as jnp
from jax import lax
from jax.experimental import pallas as pl
from jax.experimental.pallas import tpu as pltpu
from jax.sharding import PartitionSpec as P

HEADS = 8
HD = 72
WIDTH = HEADS * HD
SLOT = 256
NX, NZ, NY = 4, 8, 4
F32 = jnp.float32
BF16 = jnp.bfloat16
SCALE = 1.0 / HD**0.5

CHUNKS = [(0, 48), (48, 48), (96, 48), (144, 48), (192, 64)]
STEPS = ("z1", "x1", "z3", "x3", "z7")
ROUTE = [
    (slot, slot * SLOT + row, rows, tuple(STEPS[(i + k) % 5] for k in range(5)))
    for slot in range(2)
    for i, (row, rows) in enumerate(CHUNKS)
]
NC = len(ROUTE)
HALF_A = 80


def window(head):
    low = head * HD // 128 * 128
    return low, min((head * HD + HD + 127) // 128 * 128, WIDTH)


def nt(a, b):
    return lax.dot_general(a, b, (((1,), (1,)), ((), ())), preferred_element_type=F32)


def nn(a, b):
    return jnp.dot(a, b, preferred_element_type=F32)


def tn(a, b):
    return lax.dot_general(a, b, (((0,), (0,)), ((), ())), preferred_element_type=F32)


def kernel(
    len_ref,
    tgt_ref,
    x_ref,
    g_ref,
    b_ref,
    w_ref,
    qb_ref,
    og_ref,
    ao_ref,
    pg_ref,
    wg_ref,
    gg_ref,
    bg_ref,
    qg_ref,
    wf,
    xh,
    nrm,
    nrmt,
    rs,
    qkv,
    ks,
    probs,
    do,
    dqkv,
    o,
    s1,
    r1,
    s2,
    r2,
    part,
    rc,
    a1,
    b1,
    a2,
    b2,
    ta,
    tb,
    gsum,
    rx,
    xs,
    rz,
    full,
    vs,
    vr,
    vx,
    vz,
    route_sem,
    ag_sem,
    rs_sem,
    ar_sem,
    v_sem,
):
    dp = lax.axis_index("dp")
    fs = lax.axis_index("fsdp")
    z, x = dp // NX, dp % NX
    y, c = fs // 2, fs % 2
    partner = {
        "x1": z * NX + (x + 1 - 2 * (x % 2)),
        "x3": z * NX + (3 - x),
        "z1": (z + 1 - 2 * (z % 2)) * NX + x,
        "z3": ((z // 4) * 4 + 3 - z % 4) * NX + x,
        "z7": (7 - z) * NX + x,
    }
    y1, y2, y3 = y + 1 - 2 * (y % 2), (y + 2) % NY, 3 - y
    sib = (dp, y * 2 + 1 - c)
    at_y1 = (dp, y1 * 2 + c)
    at_y3 = (dp, y3 * 2 + c)
    at_x = [None] + [(z * NX + (x + j) % NX, fs) for j in range(1, NX)]
    at_z = [None] + [((z + j) % NZ * NX + x, fs) for j in range(1, NZ)]

    def remote(src, dst, send, recv, where):
        return pltpu.make_async_remote_copy(
            src_ref=src,
            dst_ref=dst,
            send_sem=send,
            recv_sem=recv,
            device_id=where,
            device_id_type=pl.DeviceIdType.MESH,
        )

    barrier = pltpu.get_barrier_semaphore()
    peers = [sib, at_y1, at_y3] + at_x[1:] + at_z[1:]
    for peer in peers:
        pl.semaphore_signal(barrier, inc=1, device_id=peer, device_id_type=pl.DeviceIdType.MESH)
    wf[pl.ds(fs * 144, 144), :] = w_ref[...]
    pl.semaphore_wait(barrier, len(peers))

    pending = []

    def start(copy):
        copy.start()
        pending.append(copy)
        return copy

    flip = []
    for slot in range(2):
        mask = jnp.bitwise_xor(tgt_ref[slot], dp)
        bits = [jnp.bitwise_and(jnp.right_shift(mask, i), 1) for i in range(5)]
        flip.append(
            {
                "x1": jnp.bitwise_xor(bits[0], bits[1]) == 1,
                "x3": bits[1] == 1,
                "z1": jnp.bitwise_xor(bits[2], bits[3]) == 1,
                "z3": jnp.bitwise_xor(bits[3], bits[4]) == 1,
                "z7": bits[4] == 1,
            }
        )

    def route(which, first, sbuf, rbuf, last):
        def source(i, k):
            _, row, rows, _ = ROUTE[i]
            ref = first if k == 0 else sbuf.at[k - 1]
            return ref.at[pl.ds(row, rows), :]

        copies = {}

        def send(i, k):
            _, row, rows, order = ROUTE[i]
            copies[i, k] = start(
                remote(
                    source(i, k),
                    rbuf.at[k, pl.ds(row, rows), :],
                    route_sem.at[which, 0, i, k],
                    route_sem.at[which, 1, i, k],
                    (partner[order[k]], fs),
                )
            )

        def advance(i, k):
            slot, row, rows, order = ROUTE[i]
            copies[i, k].wait_recv()
            value = jnp.where(
                flip[slot][order[k]], rbuf[k, pl.ds(row, rows), :], source(i, k)[...]
            )
            if k < 4:
                sbuf[k, pl.ds(row, rows), :] = value
                send(i, k + 1)
            else:
                last[pl.ds(row, rows), :] = value

        return send, advance

    send1, advance1 = route(0, og_ref, s1, r1, do)
    send2, advance2 = route(1, o, s2, r2, ao_ref)

    def ag(i, src, row, rows, where):
        return start(
            remote(src, wf.at[pl.ds(row, rows), :], ag_sem.at[0, i], ag_sem.at[1, i], where)
        )

    rest = 144 - HALF_A
    own = fs * 144
    row1, row2, row3 = (y1 * 2 + c) * 144, (y2 * 2 + c) * 144, (y3 * 2 + c) * 144
    head_rows, tail_rows = w_ref.at[pl.ds(0, HALF_A), :], w_ref.at[pl.ds(HALF_A, rest), :]

    def rows_of(row, rows):
        return wf.at[pl.ds(row, rows), :]

    ag_a0 = ag(0, head_rows, own, HALF_A, at_y1)
    ag_b0 = ag(1, tail_rows, own + HALF_A, rest, at_y3)
    for i in range(0, NC // 2):
        send1(i, 0)
        send1(i + NC // 2, 0)
    ag_a1 = ag(2, tail_rows, own + HALF_A, rest, at_y1)
    ag_b1 = ag(3, head_rows, own, HALF_A, at_y3)
    to_sib = [ag(4, w_ref, own, 144, sib)]

    def ag_relay():
        ag_a0.wait_recv()
        relay_a = ag(5, rows_of(row1, HALF_A), row1, HALF_A, at_y3)
        to_sib.append(ag(7, rows_of(row1, HALF_A), row1, HALF_A, sib))
        ag_b0.wait_recv()
        relay_b = ag(6, rows_of(row3 + HALF_A, rest), row3 + HALF_A, rest, at_y1)
        to_sib.append(ag(8, rows_of(row3 + HALF_A, rest), row3 + HALF_A, rest, sib))
        return relay_a, relay_b

    def ag_second():
        ag_a1.wait_recv()
        to_sib.append(ag(9, rows_of(row1 + HALF_A, rest), row1 + HALF_A, rest, sib))
        ag_b1.wait_recv()
        to_sib.append(ag(10, rows_of(row3, HALF_A), row3, HALF_A, sib))

    def ag_third(relays):
        relays[0].wait_recv()
        to_sib.append(ag(11, rows_of(row2, HALF_A), row2, HALF_A, sib))
        relays[1].wait_recv()
        to_sib.append(ag(12, rows_of(row2 + HALF_A, rest), row2 + HALF_A, rest, sib))
        for copy in to_sib:
            copy.wait_recv()

    def norm(slot):
        def step(i, _):
            rows = pl.ds(pl.multiple_of(slot * SLOT + i * 32, 32), 32)
            v = x_ref[rows, :].astype(F32)
            v = v - jnp.mean(v, axis=-1, keepdims=True)
            inv = lax.rsqrt(jnp.mean(v * v, axis=-1, keepdims=True) + 1e-6)
            v = v * inv
            xh[rows, :] = v
            rs[rows, :] = jnp.broadcast_to(inv, (32, 128))
            nrm[rows, :] = (v * g_ref[...] + b_ref[...]).astype(BF16)
            return 0

        lax.fori_loop(0, SLOT // 32, step, 0)

    def transpose():
        for slot in range(2):
            rows = slice(slot * SLOT, slot * SLOT + SLOT)
            nrmt[:, rows] = nrm[rows, :].T

    def project(slot):
        rows = slice(slot * SLOT, slot * SLOT + SLOT)
        qkv[rows, :] = (nn(nrm[rows, :], wf[...]) + qb_ref[...]).astype(BF16)
        ks[rows, :] = qkv[rows, WIDTH : 2 * WIDTH]

    def lanes(head):
        low, high = window(head)
        lane = lax.broadcasted_iota(jnp.int32, (1, high - low), 1) + low
        inside = (lane >= head * HD) & (lane < head * HD + HD)
        return inside.astype(F32).astype(BF16)

    def tiles_add(store, head, value):
        low, high = window(head)
        for t in range(low, high, 128):
            piece = value[:, t - low : min(t + 128, high) - low]
            store[t] = store[t] + piece if t in store else piece

    def forward(slot):
        rows = slice(slot * SLOT, slot * SLOT + SLOT)
        length = len_ref[slot]
        live_row = lax.broadcasted_iota(jnp.int32, (SLOT, 1), 0) < length
        out = {}
        for head in range(HEADS):
            low, high = window(head)
            mine = lanes(head)
            q = qkv[rows, low:high] * mine
            k = ks[rows, low:high]
            v = qkv[rows, 2 * WIDTH + low : 2 * WIDTH + high] * mine
            s = nt(k, q) * SCALE
            s = jnp.where(live_row, s, -1e30)
            e = jnp.exp(s - jnp.max(s, axis=0, keepdims=True))
            p = e / jnp.sum(e, axis=0, keepdims=True)
            probs[slot * HEADS + head] = p
            tiles_add(out, head, tn(p.astype(BF16), v).astype(BF16))
        for t, value in out.items():
            value = jnp.where(live_row, value.astype(F32), 0.0).astype(BF16)
            o[rows, t : t + value.shape[1]] = value

    def backward(slot, after):
        rows = slice(slot * SLOT, slot * SLOT + SLOT)
        length = len_ref[slot]
        live_row = lax.broadcasted_iota(jnp.int32, (SLOT, 1), 0) < length
        do[rows, :] = jnp.where(live_row, do[rows, :].astype(F32), 0.0).astype(BF16)
        gq, gk, gv = {}, {}, {}
        for head in range(HEADS):
            low, high = window(head)
            mine = lanes(head)
            q = qkv[rows, low:high] * mine
            k = ks[rows, low:high] * mine
            v = qkv[rows, 2 * WIDTH + low : 2 * WIDTH + high]
            up = do[rows, low:high] * mine
            p = probs[slot * HEADS + head]
            tiles_add(gv, head, nn(p.astype(BF16), up).astype(BF16))
            gp = nt(v, up)
            delta = jnp.sum(gp * p, axis=0, keepdims=True)
            gs = (p * (gp - delta) * SCALE).astype(BF16)
            tiles_add(gk, head, nn(gs, q).astype(BF16))
            tiles_add(gq, head, tn(gs, k).astype(BF16))
            after(slot, head)
        for t, value in gq.items():
            dqkv[rows, t : t + value.shape[1]] = value
        gk = jnp.concatenate([gk[t] for t in sorted(gk)], axis=1)
        dqkv[rows, WIDTH : 2 * WIDTH] = gk
        for t, value in gv.items():
            dqkv[rows, 2 * WIDTH + t : 2 * WIDTH + t + value.shape[1]] = value

    def weight_block(owner):
        return nn(nrmt[pl.ds(pl.multiple_of(owner * 144, 16), 144), :], dqkv[...])

    def put_block(par, j, value, extra):
        for t in range(14):
            piece = value[:, t * 128 : min(t * 128 + 128, 3 * WIDTH)]
            wide = piece.shape[1]
            if extra is not None:
                piece = piece + extra[j, pl.ds(t * 144, 144), 0:wide].astype(F32)
            part[par, j, pl.ds(t * 144, 144), 0:wide] = piece.astype(BF16)

    def rs_copy(i, src, dst, where):
        return remote(src, dst, rs_sem.at[0, i], rs_sem.at[1, i], where)

    def weights_for_sibling():
        def step(j, _):
            put_block(1 - c, j, weight_block(j * 2 + 1 - c), None)
            rs_copy(j, part.at[1 - c, j], rc.at[j], sib).start()
            return 0

        lax.fori_loop(0, NY, step, 0)

    def weights_own(order):
        out = {}
        for i, j in enumerate(order):
            rs_copy(j, part.at[1 - c, j], rc.at[j], sib).wait_recv()
            put_block(c, j, weight_block(j * 2 + c), rc)
            low, high = part.at[c, j, pl.ds(0, 1024), :], part.at[c, j, pl.ds(1024, 1024), :]
            if i == 0:
                out["a0"] = start(rs_copy(4, low, a1.at[0], at_y1))
                out["b0"] = start(rs_copy(5, high, b1.at[0], at_y3))
            elif i == 1:
                out["a1"] = start(rs_copy(6, low, a1.at[1], at_y1))
            elif i == 2:
                out["b1"] = start(rs_copy(7, high, b1.at[1], at_y3))
        return out

    def add(*terms):
        total = terms[0].astype(F32)
        for term in terms[1:]:
            total = total + term.astype(F32)
        return total

    def reduce_second(copies):
        copies["a0"].wait_recv()
        ta[...] = add(part[c, y3, pl.ds(0, 1024), :], a1[0]).astype(BF16)
        copies["a2"] = start(rs_copy(8, ta, a2, at_y3))
        copies["b0"].wait_recv()
        tb[...] = add(part[c, y1, pl.ds(1024, 1024), :], b1[0]).astype(BF16)
        copies["b2"] = start(rs_copy(9, tb, b2, at_y1))

    def reduce_last(copies):
        copies["a1"].wait_recv()
        copies["a2"].wait_recv()
        gsum[pl.ds(0, 1024), :] = add(part[c, y, pl.ds(0, 1024), :], a1[1], a2[...]).astype(BF16)
        copies["b1"].wait_recv()
        copies["b2"].wait_recv()
        gsum[pl.ds(1024, 1024), :] = add(part[c, y, pl.ds(1024, 1024), :], b1[1], b2[...]).astype(
            BF16
        )

    def ar_copy(i, src, dst, where):
        return start(remote(src, dst, ar_sem.at[0, i], ar_sem.at[1, i], where))

    def ar_x_send():
        return [
            ar_copy(j - 1, gsum.at[pl.ds((x + j) % NX * 512, 512), :], rx.at[j - 1], at_x[j])
            for j in range(1, NX)
        ]

    def ar_z_send(copies):
        for copy in copies:
            copy.wait_recv()
        xs[...] = add(gsum[pl.ds(x * 512, 512), :], rx[0], rx[1], rx[2]).astype(BF16)
        return [
            ar_copy(2 + j, xs.at[pl.ds((z + j) % NZ * 64, 64), :], rz.at[j - 1], at_z[j])
            for j in range(1, NZ)
        ]

    def ar_z_gather(copies):
        for copy in copies:
            copy.wait_recv()
        here = pl.ds(x * 512 + z * 64, 64)
        full[here, :] = add(xs[pl.ds(z * 64, 64), :], *[rz[j] for j in range(7)]).astype(BF16)
        return [ar_copy(9 + j, full.at[here, :], full.at[here, :], at_z[j]) for j in range(1, NZ)]

    def ar_x_gather(copies):
        for copy in copies:
            copy.wait_recv()
        here = pl.ds(x * 512, 512)
        return [ar_copy(16 + j, full.at[here, :], full.at[here, :], at_x[j]) for j in range(1, NX)]

    def v_copy(i, src, dst, where):
        return start(remote(src, dst, v_sem.at[0, i], v_sem.at[1, i], where))

    def v_pair(i, where):
        return v_copy(i, vs.at[i], vr.at[i], where)

    def v_next(i, copy):
        copy.wait_recv()
        vs[i + 1] = vs[i] + vr[i]

    def v_x_send():
        vx[x] = vs[3]
        return [v_copy(2 + j, vs.at[3], vx.at[x], at_x[j]) for j in range(1, NX)]

    def v_z_send(copies):
        for copy in copies:
            copy.wait_recv()
        total = vx[0] + vx[1] + vx[2] + vx[3]
        vs[4] = total
        vz[z] = total
        return [v_copy(5 + j, vs.at[4], vz.at[z], at_z[j]) for j in range(1, NZ)]

    def v_last(copies):
        for copy in copies:
            copy.wait_recv()
        total = vz[0]
        for j in range(1, NZ):
            total = total + vz[j]
        gg_ref[...] = total[:, 0:1152]
        bg_ref[...] = total[:, 1152:2304]
        qg_ref[...] = total[:, 2304:4032]

    def input_gradient():
        def step(i, carry):
            rows = pl.ds(pl.multiple_of(i * SLOT, SLOT), SLOT)
            probs_rows = nt(dqkv[rows, :], wf[...]).astype(BF16)
            nrm[rows, :] = probs_rows
            return carry

        lax.fori_loop(0, 2, step, 0)

        def piece(i, carry):
            gsum_, bsum_, qsum_ = carry
            rows = pl.ds(pl.multiple_of(i * 32, 32), 32)
            dn = nrm[rows, :].astype(F32)
            h = xh[rows, :]
            gsum_ = gsum_ + jnp.sum(dn * h, axis=0, keepdims=True)
            bsum_ = bsum_ + jnp.sum(dn, axis=0, keepdims=True)
            qsum_ = qsum_ + jnp.sum(dqkv[rows, :].astype(F32), axis=0, keepdims=True)
            d = dn * g_ref[...]
            m1 = jnp.mean(d, axis=-1, keepdims=True)
            m2 = jnp.mean(d * h, axis=-1, keepdims=True)
            pg_ref[rows, :] = (rs[rows, 0:1] * (d - m1 - h * m2)).astype(BF16)
            return gsum_, bsum_, qsum_

        zero = (jnp.zeros((1, 1152), F32), jnp.zeros((1, 1152), F32), jnp.zeros((1, 1728), F32))
        gsum_, bsum_, qsum_ = lax.fori_loop(0, 16, piece, zero)
        vs[0, :, 0:1152] = gsum_
        vs[0, :, 1152:2304] = bsum_
        vs[0, :, 2304:4032] = qsum_
        vs[0, :, 4032:4096] = jnp.zeros((1, 64), F32)

    def advance_all(advance, k):
        for i in range(NC // 2):
            advance(i, k)
            advance(i + NC // 2, k)

    for par in range(2):
        for j in range(NY):
            part[par, j, pl.ds(2016, 32), :] = jnp.zeros((32, 128), BF16)
            part[par, j, pl.ds(13 * 144, 144), :] = jnp.zeros((144, 128), BF16)
    norm(0)
    relays = ag_relay()
    norm(1)
    advance_all(advance1, 0)
    ag_second()
    transpose()
    advance_all(advance1, 1)
    ag_third(relays)
    project(0)
    advance_all(advance1, 2)
    project(1)
    forward(0)
    advance_all(advance1, 3)
    forward(1)
    advance_all(advance1, 4)
    for i in range(NC // 2):
        send2(i, 0)
        send2(i + NC // 2, 0)

    def after(slot, head):
        if slot == 1:
            for i in range(NC):
                if i * HEADS // NC == head:
                    advance2(i, 0)

    backward(0, after)
    backward(1, after)
    weights_for_sibling()
    for i in range(NC // 2):
        advance2(i, 1)
        advance2(i + NC // 2, 1)
    copies = weights_own((y2, y1, y3, y))
    input_gradient()
    va = v_pair(0, sib)
    advance_all(advance2, 2)
    v_next(0, va)
    va = v_pair(1, at_y1)
    reduce_second(copies)
    advance_all(advance2, 3)
    v_next(1, va)
    va = v_pair(2, at_y3)
    reduce_last(copies)
    ar = ar_x_send()
    v_next(2, va)
    vc = v_x_send()
    advance_all(advance2, 4)
    ar = ar_z_send(ar)
    vc = v_z_send(vc)
    ar = ar_z_gather(ar)
    ar = ar_x_gather(ar)
    v_last(vc)
    for copy in ar:
        copy.wait_recv()
    for t in range(14):
        wide = min(128, 3 * WIDTH - t * 128)
        wg_ref[:, t * 128 : t * 128 + wide] = full[pl.ds(t * 144, 144), 0:wide].astype(F32)
    for j in range(NY):
        rs_copy(j, part.at[1 - c, j], rc.at[j], sib).wait_send()
    for copy in pending:
        copy.wait_send()


def body(patches, layer_norm_gain, layer_norm_bias, w_qkv, qkv_bias, out_grad, lengths, target):
    rows, depth = patches.shape
    cols = w_qkv.shape[1]
    full_rows = 8 * w_qkv.shape[0]
    vmem = pl.BlockSpec(memory_space=pltpu.VMEM)
    smem = pl.BlockSpec(memory_space=pltpu.SMEM)
    shape = jax.ShapeDtypeStruct
    out = pl.pallas_call(
        kernel,
        out_shape=(
            shape((rows, WIDTH), BF16),
            shape((rows, depth), BF16),
            shape(w_qkv.shape, F32),
            shape((1, depth), F32),
            shape((1, depth), F32),
            shape((1, cols), F32),
        ),
        in_specs=[smem, smem] + [vmem] * 6,
        out_specs=[vmem] * 6,
        scratch_shapes=[
            pltpu.VMEM((full_rows, cols), BF16),
            pltpu.VMEM((rows, depth), F32),
            pltpu.VMEM((rows, depth), BF16),
            pltpu.VMEM((depth, rows), BF16),
            pltpu.VMEM((rows, 128), F32),
            pltpu.VMEM((rows, cols), BF16),
            pltpu.VMEM((rows, WIDTH), BF16),
            pltpu.VMEM((2 * HEADS, SLOT, SLOT), F32),
            pltpu.VMEM((rows, WIDTH), BF16),
            pltpu.VMEM((rows, cols), BF16),
            pltpu.VMEM((rows, WIDTH), BF16),
            pltpu.VMEM((4, rows, WIDTH), BF16),
            pltpu.VMEM((5, rows, WIDTH), BF16),
            pltpu.VMEM((4, rows, WIDTH), BF16),
            pltpu.VMEM((5, rows, WIDTH), BF16),
            pltpu.VMEM((2, NY, 2048, 128), BF16),
            pltpu.VMEM((NY, 2048, 128), BF16),
            pltpu.VMEM((2, 1024, 128), BF16),
            pltpu.VMEM((2, 1024, 128), BF16),
            pltpu.VMEM((1024, 128), BF16),
            pltpu.VMEM((1024, 128), BF16),
            pltpu.VMEM((1024, 128), BF16),
            pltpu.VMEM((1024, 128), BF16),
            pltpu.VMEM((2048, 128), BF16),
            pltpu.VMEM((3, 512, 128), BF16),
            pltpu.VMEM((512, 128), BF16),
            pltpu.VMEM((7, 64, 128), BF16),
            pltpu.VMEM((2048, 128), BF16),
            pltpu.VMEM((5, 1, 4096), F32),
            pltpu.VMEM((3, 1, 4096), F32),
            pltpu.VMEM((NX, 1, 4096), F32),
            pltpu.VMEM((NZ, 1, 4096), F32),
            pltpu.SemaphoreType.DMA((2, 2, NC, 5)),
            pltpu.SemaphoreType.DMA((2, 13)),
            pltpu.SemaphoreType.DMA((2, 10)),
            pltpu.SemaphoreType.DMA((2, 20)),
            pltpu.SemaphoreType.DMA((2, 13)),
        ],
        compiler_params=pltpu.CompilerParams(
            collective_id=0, has_side_effects=True, vmem_limit_bytes=58 * 1024 * 1024
        ),
    )(
        lengths,
        target,
        patches,
        layer_norm_gain[None],
        layer_norm_bias[None],
        w_qkv,
        qkv_bias[None],
        out_grad,
    )
    attn_out, patch_gradient, weight_grad, gain, bias, qbias = out
    return attn_out, patch_gradient, weight_grad, gain[0], bias[0], qbias[0]


def solution(mesh):
    return jax.shard_map(
        body,
        mesh=mesh,
        in_specs=(
            P(("dp", "fsdp"), None),
            P(),
            P(),
            P("fsdp", None),
            P(),
            P(("dp", "fsdp"), None),
            P(("dp", "fsdp")),
            P(("dp", "fsdp")),
        ),
        out_specs=(
            P(("dp", "fsdp"), None),
            P(("dp", "fsdp"), None),
            P("fsdp", None),
            P(),
            P(),
            P(),
        ),
        check_vma=False,
    )
```

time: 939 us -> 141 us (0.15)
  waiting for transfers between devices: 632 us -> 0 us
  blocking collectives: 157 us -> 0 us
  Pallas kernels: 0 us -> 128 us
  matrix products: 44.2 us -> 0 us
  other arithmetic: 44.8 us -> 1.86 us
  starting transfers between devices: 22.5 us -> 0 us
  between operations: 15.1 us -> 0.68 us
    ppermute x10 -> x0, waiting for transfers between devices: 453 us -> none  [swapped(): return lax.ppermute(value, axis, pairs)]
    psum x1 -> x0, waiting for transfers between devices: 142 us -> none  [body(): weight_grad = lax.psum(owned, 'dp').astype(jnp.float32)]
    pallas_call x0 -> x1, Pallas kernels: none -> 128 us  [body(): pl.pallas_call(kernel, out_shape=(shape((rows, WIDTH), BF16), shape((rows...]
    unnamed x1 -> x0, blocking collectives: 81.8 us -> none
    psum x1 -> x0, blocking collectives: 75 us -> none  [body(): lax.psum((partial_gain_gradient, partial_bias, partial_qbias), ('dp', 'fs...]
    dot_general x8 -> x0, matrix products: 39.7 us -> none  [the longest x1 8.05 us: attend(): jnp.einsum('hqk,khd->qhd', grad_scores, keys, preferred_element_type=jnp....]
    all_gather x1 -> x0, waiting for transfers between devices: 36.2 us -> none  [body(): full_weight = lax.all_gather(w_qkv, 'fsdp', axis=0, tiled=True)]
    ppermute x10 -> x0, starting transfers between devices: 22.1 us -> none  [swapped(): return lax.ppermute(value, axis, pairs)]
  transfers between devices with their start and end apart: 13 -> 0, of which waited for: 11 -> 0; matrix products, arithmetic and copies ran while one was open for 2% -> 0% of each run, Pallas kernels for 0% -> 0%
where the time goes in v1:
time: 141 us
  Pallas kernels  128 us (91%)
  local copies, waits for them, and re-layouts  10.9 us (8%)
  other arithmetic  1.86 us (1%)
    pallas_call x1, Pallas kernels, body(): pl.pallas_call(kernel, out_shape=(shape((rows, WIDTH), BF16), shape((rows...  128 us
    unnamed x14, local copies, waits for them, and re-layouts  6.99 us

profile of v1, /device:TPU:8, one launch (start us, length us, event | category | flops | bytes accessed | tf_op | source)
XLA Modules:
  0.0 141.0 jit_solution(104962492710426578)
XLA Ops:
  0.6 1.3 broadcast_in_dim.9.g_ref
  1.9 1.3 broadcast_in_dim.10.b_ref
  3.2 1.3 broadcast_in_dim.11.qb_ref
  4.5 2.1 %copy.14.og_ref = bf16[512,576]{1,0:T(8,128)(2,1)} copy(bf16[512,576]{0,1:T(8,128)(2,1)} %param.13) | data formatting | bytes 1179648 | tf_op args[5]
  6.7 127.6 %shard_map.127 = (bf16[512,576]{1,0:T(8,128)(2,1)}, bf16[512,1152]{1,0:T(8,128)(2,1)}, f32[144,1728]{1,0:T(8,128)}, f32[1,1152]{1,0:T(1,128)}, f32[1,1152]{1,0:T(1,128)}, /*index=5*/f32[1,1728]{1,0:T(1,128)}) custom-call(s32[2]{0:T(128)} %len_ref.1, s32[2]{0:T(128)} %tgt_ref.1, bf16[512,1152]{1,0:T(8,128)(2,1)} %x_ref.1, f32[1,1152]{1,0:T(1,128)} %broadcast_in_dim.9.g_ref, ...), custom_call_target="tpu_custom_call" | custom-call | tf_op jit(solution)/shard_map/pallas_call | solution.py:553
  134.3 0.0 copy-start.4
  134.3 0.0 copy-start.3
  134.3 0.0 copy-start.2
  134.3 0.0 copy-start
  134.3 2.2 %copy.15 = bf16[512,576]{0,1:T(8,128)(2,1)} copy(bf16[512,576]{1,0:T(8,128)(2,1)} %get-tuple-element.18) | data formatting | bytes 1179648
  136.5 0.0 copy-done.4
  136.5 0.6 reduce
  137.2 0.0 copy-done.3
  137.2 0.6 reduce.1
  137.8 0.0 copy-done.2
  137.8 0.6 reduce.2
  138.4 0.0 copy-done
  138.4 0.0 copy-start.1
  138.4 1.0 copy.18
  139.4 0.6 copy-done.1
  140.0 1.0 copy.19
Async XLA Ops:
  134.3 2.3 %copy-start.4 = (f32[1,1152]{1,0:T(1,128)S(1)}, f32[1,1152]{1,0:T(1,128)}, u32[]{:S(2)}) copy-start(f32[1,1152]{1,0:T(1,128)} %get-tuple-element.15) | copy-start | bytes 13828
  134.3 2.9 %copy-start.3 = (f32[1,1152]{1,0:T(1,128)S(1)}, f32[1,1152]{1,0:T(1,128)}, u32[]{:S(2)}) copy-start(f32[1,1152]{1,0:T(1,128)} %get-tuple-element.16) | copy-start | bytes 13828
  134.3 3.5 %copy-start.2 = (f32[1,1728]{1,0:T(1,128)S(1)}, f32[1,1728]{1,0:T(1,128)}, u32[]{:S(2)}) copy-start(f32[1,1728]{1,0:T(1,128)} %get-tuple-element.17) | copy-start | bytes 20740
  134.3 4.1 %copy-start = (bf16[512,1152]{1,0:T(8,128)(2,1)S(1)}, bf16[512,1152]{1,0:T(8,128)(2,1)}, u32[]{:S(2)}) copy-start(bf16[512,1152]{1,0:T(8,128)(2,1)} %get-tuple-element.31) | copy-start | bytes 3538948
  138.4 1.6 %copy-start.1 = (f32[144,1728]{1,0:T(8,128)S(1)}, f32[144,1728]{1,0:T(8,128)}, u32[]{:S(2)}) copy-start(f32[144,1728]{1,0:T(8,128)} %get-tuple-element.32) | copy-start | bytes 2985988

commit v2 on v1

--- a/solution.py
+++ b/solution.py
@@ -14,13 +14,35 @@
 BF16 = jnp.bfloat16
 SCALE = 1.0 / HD**0.5
 
-CHUNKS = [(0, 48), (48, 48), (96, 48), (144, 48), (192, 64)]
-STEPS = ("z1", "x1", "z3", "x3", "z7")
-ROUTE = [
-    (slot, slot * SLOT + row, rows, tuple(STEPS[(i + k) % 5] for k in range(5)))
-    for slot in range(2)
-    for i, (row, rows) in enumerate(CHUNKS)
-]
+SWAPS = (
+    (
+        (-16711936, -16776961),
+        (1717960704, -1717960705),
+        (-65536, -1),
+        (1717960704, -1717960705),
+    ),
+    (
+        (1717960704, -1717960705),
+        (-256, -1),
+        (1717960704, -1717960705),
+        (-16777216, -16776961),
+    ),
+)
+CHUNK = WIDTH // 6
+
+
+def chunk_steps(i):
+    net = i % 2
+    steps = [("z", net, s) for s in range(4)]
+    first, second = (("x", 1), ("x", 3)) if i // 2 % 2 == 0 else (("x", 3), ("x", 1))
+    at = i % 3
+    steps.insert(at, first)
+    steps.insert(at + 3, second)
+    return tuple(steps)
+
+
+ROUTE = [(slot, i * CHUNK, CHUNK, chunk_steps(i)) for slot in range(2) for i in range(6)]
+HOPS = 6
 NC = len(ROUTE)
 HALF_A = 80
 
@@ -45,18 +67,20 @@
 def kernel(
     len_ref,
     tgt_ref,
-    x_ref,
+    x_hbm,
     g_ref,
     b_ref,
-    w_ref,
+    w_hbm,
     qb_ref,
+    og_hbm,
+    ao_hbm,
+    pg_hbm,
+    full,
+    sums_ref,
+    x_ref,
     og_ref,
     ao_ref,
     pg_ref,
-    wg_ref,
-    gg_ref,
-    bg_ref,
-    qg_ref,
     wf,
     xh,
     nrm,
@@ -84,7 +108,6 @@
     rx,
     xs,
     rz,
-    full,
     vs,
     vr,
     vx,
@@ -94,18 +117,18 @@
     rs_sem,
     ar_sem,
     v_sem,
+    io_sem,
 ):
     dp = lax.axis_index("dp")
     fs = lax.axis_index("fsdp")
     z, x = dp // NX, dp % NX
     y, c = fs // 2, fs % 2
-    partner = {
-        "x1": z * NX + (x + 1 - 2 * (x % 2)),
-        "x3": z * NX + (3 - x),
-        "z1": (z + 1 - 2 * (z % 2)) * NX + x,
-        "z3": ((z // 4) * 4 + 3 - z % 4) * NX + x,
-        "z7": (7 - z) * NX + x,
-    }
+    even = (z + 1 - 2 * (z % 2)) * NX + x
+    odd = (z + NZ - 1 + 2 * (z % 2)) % NZ * NX + x
+    partner = {("x", 1): z * NX + (x + 1 - 2 * (x % 2)), ("x", 3): z * NX + (3 - x)}
+    for net in range(2):
+        for stage in range(4):
+            partner["z", net, stage] = odd if (net + stage) % 2 else even
     y1, y2, y3 = y + 1 - 2 * (y % 2), (y + 2) % NY, 3 - y
     sib = (dp, y * 2 + 1 - c)
     at_y1 = (dp, y1 * 2 + c)
@@ -123,11 +146,18 @@
             device_id_type=pl.DeviceIdType.MESH,
         )
 
+    load_og = pltpu.make_async_copy(og_hbm, og_ref, io_sem.at[0])
+    load_w = pltpu.make_async_copy(w_hbm, wf.at[pl.ds(fs * 144, 144), :], io_sem.at[1])
+    load_x = pltpu.make_async_copy(x_hbm, x_ref, io_sem.at[2])
+    load_w.start()
+    load_og.start()
+    load_x.start()
     barrier = pltpu.get_barrier_semaphore()
     peers = [sib, at_y1, at_y3] + at_x[1:] + at_z[1:]
     for peer in peers:
         pl.semaphore_signal(barrier, inc=1, device_id=peer, device_id_type=pl.DeviceIdType.MESH)
-    wf[pl.ds(fs * 144, 144), :] = w_ref[...]
+    load_w.wait()
+    load_og.wait()
     pl.semaphore_wait(barrier, len(peers))
 
     pending = []
@@ -140,31 +170,38 @@
     flip = []
     for slot in range(2):
         mask = jnp.bitwise_xor(tgt_ref[slot], dp)
-        bits = [jnp.bitwise_and(jnp.right_shift(mask, i), 1) for i in range(5)]
-        flip.append(
-            {
-                "x1": jnp.bitwise_xor(bits[0], bits[1]) == 1,
-                "x3": bits[1] == 1,
-                "z1": jnp.bitwise_xor(bits[2], bits[3]) == 1,
-                "z3": jnp.bitwise_xor(bits[3], bits[4]) == 1,
-                "z7": bits[4] == 1,
-            }
-        )
+        bits = [jnp.bitwise_and(jnp.right_shift(mask, i), 1) for i in range(2)]
+        zmask = jnp.right_shift(mask, 2)
+        shift = jnp.bitwise_and(zmask, 3) * 8 + z
+        swap = {
+            ("x", 1): jnp.bitwise_xor(bits[0], bits[1]) == 1,
+            ("x", 3): bits[1] == 1,
+        }
+        for net in range(2):
+            for stage in range(4):
+                low, high = SWAPS[net][stage]
+                word = jnp.where(zmask < 4, jnp.int32(low), jnp.int32(high))
+                swap["z", net, stage] = jnp.bitwise_and(jnp.right_shift(word, shift), 1) == 1
+        flip.append(swap)
 
     def route(which, first, sbuf, rbuf, last):
+        def place(ref, i):
+            slot, row, rows, _ = ROUTE[i]
+            if len(ref.shape) == 2:
+                return ref.at[pl.ds(row, rows), pl.ds(slot * SLOT, SLOT)]
+            return ref.at[slot, pl.ds(row, rows), :]
+
         def source(i, k):
-            _, row, rows, _ = ROUTE[i]
-            ref = first if k == 0 else sbuf.at[k - 1]
-            return ref.at[pl.ds(row, rows), :]
+            return place(first if k == 0 else sbuf.at[k - 1], i)
 
         copies = {}
 
         def send(i, k):
-            _, row, rows, order = ROUTE[i]
+            order = ROUTE[i][3]
             copies[i, k] = start(
                 remote(
                     source(i, k),
-                    rbuf.at[k, pl.ds(row, rows), :],
+                    place(rbuf.at[k], i),
                     route_sem.at[which, 0, i, k],
                     route_sem.at[which, 1, i, k],
                     (partner[order[k]], fs),
@@ -172,16 +209,16 @@
             )
 
         def advance(i, k):
-            slot, row, rows, order = ROUTE[i]
+            slot, _, _, order = ROUTE[i]
             copies[i, k].wait_recv()
             value = jnp.where(
-                flip[slot][order[k]], rbuf[k, pl.ds(row, rows), :], source(i, k)[...]
+                flip[slot][order[k]], place(rbuf.at[k], i)[...], source(i, k)[...]
             )
-            if k < 4:
-                sbuf[k, pl.ds(row, rows), :] = value
+            if k < HOPS - 1:
+                place(sbuf.at[k], i)[...] = value
                 send(i, k + 1)
             else:
-                last[pl.ds(row, rows), :] = value
+                place(last, i)[...] = value
 
         return send, advance
 
@@ -196,19 +233,18 @@
     rest = 144 - HALF_A
     own = fs * 144
     row1, row2, row3 = (y1 * 2 + c) * 144, (y2 * 2 + c) * 144, (y3 * 2 + c) * 144
-    head_rows, tail_rows = w_ref.at[pl.ds(0, HALF_A), :], w_ref.at[pl.ds(HALF_A, rest), :]
+    head_rows, tail_rows = wf.at[pl.ds(own, HALF_A), :], wf.at[pl.ds(own + HALF_A, rest), :]
 
     def rows_of(row, rows):
         return wf.at[pl.ds(row, rows), :]
 
     ag_a0 = ag(0, head_rows, own, HALF_A, at_y1)
     ag_b0 = ag(1, tail_rows, own + HALF_A, rest, at_y3)
-    for i in range(0, NC // 2):
+    for i in range(NC):
         send1(i, 0)
-        send1(i + NC // 2, 0)
     ag_a1 = ag(2, tail_rows, own + HALF_A, rest, at_y1)
     ag_b1 = ag(3, head_rows, own, HALF_A, at_y3)
-    to_sib = [ag(4, w_ref, own, 144, sib)]
+    to_sib = [ag(4, wf.at[pl.ds(own, 144), :], own, 144, sib)]
 
     def ag_relay():
         ag_a0.wait_recv()
@@ -242,7 +278,7 @@
             v = v * inv
             xh[rows, :] = v
             rs[rows, :] = jnp.broadcast_to(inv, (32, 128))
-            nrm[rows, :] = (v * g_ref[...] + b_ref[...]).astype(BF16)
+            nrm[rows, :] = (v * g_ref[...].reshape(1, -1) + b_ref[...].reshape(1, -1)).astype(BF16)
             return 0
 
         lax.fori_loop(0, SLOT // 32, step, 0)
@@ -254,7 +290,7 @@
 
     def project(slot):
         rows = slice(slot * SLOT, slot * SLOT + SLOT)
-        qkv[rows, :] = (nn(nrm[rows, :], wf[...]) + qb_ref[...]).astype(BF16)
+        qkv[rows, :] = (nn(nrm[rows, :], wf[...]) + qb_ref[...].reshape(1, -1)).astype(BF16)
         ks[rows, :] = qkv[rows, WIDTH : 2 * WIDTH]
 
     def lanes(head):
@@ -263,16 +299,17 @@
         inside = (lane >= head * HD) & (lane < head * HD + HD)
         return inside.astype(F32).astype(BF16)
 
-    def tiles_add(store, head, value):
+    def tiles_add(store, head, value, axis):
         low, high = window(head)
-        for t in range(low, high, 128):
-            piece = value[:, t - low : min(t + 128, high) - low]
-            store[t] = store[t] + piece if t in store else piece
-
-    def forward(slot):
+        for n in range(low, high, 128):
+            piece = lax.slice_in_dim(value, n - low, min(n + 128, high) - low, axis=axis)
+            store[n] = store[n] + piece if n in store else piece
+
+    def forward(slot, after):
         rows = slice(slot * SLOT, slot * SLOT + SLOT)
         length = len_ref[slot]
-        live_row = lax.broadcasted_iota(jnp.int32, (SLOT, 1), 0) < length
+        live = lax.broadcasted_iota(jnp.int32, (SLOT, 1), 0) < length
+        live_lane = lax.broadcasted_iota(jnp.int32, (1, SLOT), 1) < length
         out = {}
         for head in range(HEADS):
             low, high = window(head)
@@ -280,43 +317,43 @@
             q = qkv[rows, low:high] * mine
             k = ks[rows, low:high]
             v = qkv[rows, 2 * WIDTH + low : 2 * WIDTH + high] * mine
-            s = nt(k, q) * SCALE
-            s = jnp.where(live_row, s, -1e30)
+            s = jnp.where(live, nt(k, q) * SCALE, -1e30)
             e = jnp.exp(s - jnp.max(s, axis=0, keepdims=True))
             p = e / jnp.sum(e, axis=0, keepdims=True)
             probs[slot * HEADS + head] = p
-            tiles_add(out, head, tn(p.astype(BF16), v).astype(BF16))
-        for t, value in out.items():
-            value = jnp.where(live_row, value.astype(F32), 0.0).astype(BF16)
-            o[rows, t : t + value.shape[1]] = value
+            value = jnp.where(live_lane, tn(v, p.astype(BF16)), 0.0).astype(BF16)
+            tiles_add(out, head, value, 0)
+            after(head)
+        for n, value in out.items():
+            o[slot, n : n + value.shape[0], :] = value
 
     def backward(slot, after):
         rows = slice(slot * SLOT, slot * SLOT + SLOT)
-        length = len_ref[slot]
-        live_row = lax.broadcasted_iota(jnp.int32, (SLOT, 1), 0) < length
-        do[rows, :] = jnp.where(live_row, do[rows, :].astype(F32), 0.0).astype(BF16)
+        live_lane = lax.broadcasted_iota(jnp.int32, (1, SLOT), 1) < len_ref[slot]
         gq, gk, gv = {}, {}, {}
         for head in range(HEADS):
             low, high = window(head)
             mine = lanes(head)
+            row = lax.broadcasted_iota(jnp.int32, (high - low, 1), 0) + low
+            keep = (row >= head * HD) & (row < head * HD + HD) & live_lane
             q = qkv[rows, low:high] * mine
             k = ks[rows, low:high] * mine
             v = qkv[rows, 2 * WIDTH + low : 2 * WIDTH + high]
-            up = do[rows, low:high] * mine
+            up = jnp.where(keep, do[slot, low:high, :].astype(F32), 0.0).astype(BF16)
             p = probs[slot * HEADS + head]
-            tiles_add(gv, head, nn(p.astype(BF16), up).astype(BF16))
-            gp = nt(v, up)
+            tiles_add(gv, head, nt(p.astype(BF16), up).astype(BF16), 1)
+            gp = nn(v, up)
             delta = jnp.sum(gp * p, axis=0, keepdims=True)
             gs = (p * (gp - delta) * SCALE).astype(BF16)
-            tiles_add(gk, head, nn(gs, q).astype(BF16))
-            tiles_add(gq, head, tn(gs, k).astype(BF16))
-            after(slot, head)
-        for t, value in gq.items():
-            dqkv[rows, t : t + value.shape[1]] = value
-        gk = jnp.concatenate([gk[t] for t in sorted(gk)], axis=1)
+            tiles_add(gk, head, nn(gs, q).astype(BF16), 1)
+            tiles_add(gq, head, tn(gs, k).astype(BF16), 1)
+            after(head)
+        for n, value in gq.items():
+            dqkv[rows, n : n + value.shape[1]] = value
+        gk = jnp.concatenate([gk[n] for n in sorted(gk)], axis=1)
         dqkv[rows, WIDTH : 2 * WIDTH] = gk
-        for t, value in gv.items():
-            dqkv[rows, 2 * WIDTH + t : 2 * WIDTH + t + value.shape[1]] = value
+        for n, value in gv.items():
+            dqkv[rows, 2 * WIDTH + n : 2 * WIDTH + n + value.shape[1]] = value
 
     def weight_block(owner):
         return nn(nrmt[pl.ds(pl.multiple_of(owner * 144, 16), 144), :], dqkv[...])
@@ -438,9 +475,7 @@
         total = vz[0]
         for j in range(1, NZ):
             total = total + vz[j]
-        gg_ref[...] = total[:, 0:1152]
-        bg_ref[...] = total[:, 1152:2304]
-        qg_ref[...] = total[:, 2304:4032]
+        sums_ref[...] = total
 
     def input_gradient():
         def step(i, carry):
@@ -459,7 +494,7 @@
             gsum_ = gsum_ + jnp.sum(dn * h, axis=0, keepdims=True)
             bsum_ = bsum_ + jnp.sum(dn, axis=0, keepdims=True)
             qsum_ = qsum_ + jnp.sum(dqkv[rows, :].astype(F32), axis=0, keepdims=True)
-            d = dn * g_ref[...]
+            d = dn * g_ref[...].reshape(1, -1)
             m1 = jnp.mean(d, axis=-1, keepdims=True)
             m2 = jnp.mean(d * h, axis=-1, keepdims=True)
             pg_ref[rows, :] = (rs[rows, 0:1] * (d - m1 - h * m2)).astype(BF16)
@@ -472,61 +507,86 @@
         vs[0, :, 2304:4032] = qsum_
         vs[0, :, 4032:4096] = jnp.zeros((1, 64), F32)
 
-    def advance_all(advance, k):
+    def go(advance, slot, k):
         for i in range(NC // 2):
-            advance(i, k)
-            advance(i + NC // 2, k)
+            advance(slot * (NC // 2) + i, k)
+
+    def spread(events):
+        events = list(events)
+
+        def after(head):
+            for event in events[head * len(events) // HEADS : (head + 1) * len(events) // HEADS]:
+                event[0](*event[1:])
+
+        return after
+
+    def steps(advance, slot, k):
+        return [(advance, slot * (NC // 2) + i, k) for i in range(NC // 2)]
 
     for par in range(2):
         for j in range(NY):
             part[par, j, pl.ds(2016, 32), :] = jnp.zeros((32, 128), BF16)
             part[par, j, pl.ds(13 * 144, 144), :] = jnp.zeros((144, 128), BF16)
+    load_x.wait()
     norm(0)
+    norm(1)
+    go(advance1, 0, 0)
     relays = ag_relay()
-    norm(1)
-    advance_all(advance1, 0)
+    go(advance1, 1, 0)
+    transpose()
+    go(advance1, 0, 1)
+    go(advance1, 1, 1)
     ag_second()
-    transpose()
-    advance_all(advance1, 1)
+    go(advance1, 0, 2)
+    go(advance1, 1, 2)
+    go(advance1, 0, 3)
+    go(advance1, 1, 3)
     ag_third(relays)
     project(0)
-    advance_all(advance1, 2)
+    go(advance1, 0, 4)
+    go(advance1, 1, 4)
     project(1)
-    forward(0)
-    advance_all(advance1, 3)
-    forward(1)
-    advance_all(advance1, 4)
+    forward(0, spread([]))
     for i in range(NC // 2):
         send2(i, 0)
-        send2(i + NC // 2, 0)
-
-    def after(slot, head):
-        if slot == 1:
-            for i in range(NC):
-                if i * HEADS // NC == head:
-                    advance2(i, 0)
-
-    backward(0, after)
-    backward(1, after)
+    go(advance1, 0, 5)
+    forward(1, spread([]))
+    for i in range(NC // 2):
+        send2(NC // 2 + i, 0)
+    go(advance1, 1, 5)
+    backward(0, spread(steps(advance2, 0, 0)))
+    backward(1, spread(steps(advance2, 1, 0)))
     weights_for_sibling()
-    for i in range(NC // 2):
-        advance2(i, 1)
-        advance2(i + NC // 2, 1)
+    go(advance2, 0, 1)
+    go(advance2, 1, 1)
     copies = weights_own((y2, y1, y3, y))
+    go(advance2, 0, 2)
+    go(advance2, 1, 2)
     input_gradient()
+    store_pg = pltpu.make_async_copy(pg_ref, pg_hbm, io_sem.at[0])
+    store_pg.start()
     va = v_pair(0, sib)
-    advance_all(advance2, 2)
+    go(advance2, 0, 3)
     v_next(0, va)
     va = v_pair(1, at_y1)
+    go(advance2, 1, 3)
     reduce_second(copies)
-    advance_all(advance2, 3)
     v_next(1, va)
     va = v_pair(2, at_y3)
+    go(advance2, 0, 4)
+    go(advance2, 1, 4)
     reduce_last(copies)
     ar = ar_x_send()
     v_next(2, va)
     vc = v_x_send()
-    advance_all(advance2, 4)
+    store_ao = []
+    for slot in range(2):
+        go(advance2, slot, 5)
+        copy = pltpu.make_async_copy(
+            ao_ref.at[slot], ao_hbm.at[:, pl.ds(slot * SLOT, SLOT)], io_sem.at[1 + slot]
+        )
+        copy.start()
+        store_ao.append(copy)
     ar = ar_z_send(ar)
     vc = v_z_send(vc)
     ar = ar_z_gather(ar)
@@ -534,13 +594,46 @@
     v_last(vc)
     for copy in ar:
         copy.wait_recv()
-    for t in range(14):
-        wide = min(128, 3 * WIDTH - t * 128)
-        wg_ref[:, t * 128 : t * 128 + wide] = full[pl.ds(t * 144, 144), 0:wide].astype(F32)
     for j in range(NY):
         rs_copy(j, part.at[1 - c, j], rc.at[j], sib).wait_send()
     for copy in pending:
         copy.wait_send()
+    store_pg.wait()
+    for copy in store_ao:
+        copy.wait()
+
+
+def finish(
+    ao_in, pg_in, full, sums, ao_out, pg_out, wg_ref, gg_ref, bg_ref, qg_ref, ao, pg, in_sem, out_sem
+):
+    half = pg_in.shape[0] // 2
+    pieces = [
+        (ref_in.at[rows, :], ref.at[rows, :], ref_out.at[rows, :])
+        for ref_in, ref, ref_out, rows in (
+            (pg_in, pg, pg_out, pl.ds(0, half)),
+            (pg_in, pg, pg_out, pl.ds(half, half)),
+            (ao_in, ao, ao_out, pl.ds(0, WIDTH)),
+        )
+    ]
+    loads = [
+        pltpu.make_async_copy(src, mid, in_sem.at[i]) for i, (src, mid, _) in enumerate(pieces)
+    ]
+    stores = [
+        pltpu.make_async_copy(mid, dst, out_sem.at[i]) for i, (_, mid, dst) in enumerate(pieces)
+    ]
+    for load in loads:
+        load.start()
+    for load, store in zip(loads, stores):
+        load.wait()
+        store.start()
+    for t in range(14):
+        wide = min(128, 3 * WIDTH - t * 128)
+        wg_ref[:, t * 128 : t * 128 + wide] = full[pl.ds(t * 144, 144), 0:wide].astype(F32)
+    gg_ref[...] = sums[0, 0:1152]
+    bg_ref[...] = sums[0, 1152:2304]
+    qg_ref[...] = sums[0, 2304:4032]
+    for store in stores:
+        store.wait()
 
 
 def body(patches, layer_norm_gain, layer_norm_bias, w_qkv, qkv_bias, out_grad, lengths, target):
@@ -549,20 +642,23 @@
     full_rows = 8 * w_qkv.shape[0]
     vmem = pl.BlockSpec(memory_space=pltpu.VMEM)
     smem = pl.BlockSpec(memory_space=pltpu.SMEM)
+    hbm = pl.BlockSpec(memory_space=pl.ANY)
     shape = jax.ShapeDtypeStruct
-    out = pl.pallas_call(
+    parts = pl.pallas_call(
         kernel,
         out_shape=(
-            shape((rows, WIDTH), BF16),
+            shape((WIDTH, rows), BF16),
             shape((rows, depth), BF16),
-            shape(w_qkv.shape, F32),
-            shape((1, depth), F32),
-            shape((1, depth), F32),
-            shape((1, cols), F32),
+            shape((2048, 128), BF16),
+            shape((1, 4096), F32),
         ),
-        in_specs=[smem, smem] + [vmem] * 6,
-        out_specs=[vmem] * 6,
+        in_specs=[smem, smem, hbm, vmem, vmem, hbm, vmem, hbm],
+        out_specs=[hbm, hbm, vmem, vmem],
         scratch_shapes=[
+            pltpu.VMEM((rows, depth), BF16),
+            pltpu.VMEM((WIDTH, rows), BF16),
+            pltpu.VMEM((2, WIDTH, SLOT), BF16),
+            pltpu.VMEM((rows, depth), BF16),
             pltpu.VMEM((full_rows, cols), BF16),
             pltpu.VMEM((rows, depth), F32),
             pltpu.VMEM((rows, depth), BF16),
@@ -571,13 +667,13 @@
             pltpu.VMEM((rows, cols), BF16),
             pltpu.VMEM((rows, WIDTH), BF16),
             pltpu.VMEM((2 * HEADS, SLOT, SLOT), F32),
-            pltpu.VMEM((rows, WIDTH), BF16),
+            pltpu.VMEM((2, WIDTH, SLOT), BF16),
             pltpu.VMEM((rows, cols), BF16),
-            pltpu.VMEM((rows, WIDTH), BF16),
-            pltpu.VMEM((4, rows, WIDTH), BF16),
-            pltpu.VMEM((5, rows, WIDTH), BF16),
-            pltpu.VMEM((4, rows, WIDTH), BF16),
-            pltpu.VMEM((5, rows, WIDTH), BF16),
+            pltpu.VMEM((2, WIDTH, SLOT), BF16),
+            pltpu.VMEM((5, 2, WIDTH, SLOT), BF16),
+            pltpu.VMEM((6, 2, WIDTH, SLOT), BF16),
+            pltpu.VMEM((5, 2, WIDTH, SLOT), BF16),
+            pltpu.VMEM((6, 2, WIDTH, SLOT), BF16),
             pltpu.VMEM((2, NY, 2048, 128), BF16),
             pltpu.VMEM((NY, 2048, 128), BF16),
             pltpu.VMEM((2, 1024, 128), BF16),
@@ -590,16 +686,16 @@
             pltpu.VMEM((3, 512, 128), BF16),
             pltpu.VMEM((512, 128), BF16),
             pltpu.VMEM((7, 64, 128), BF16),
-            pltpu.VMEM((2048, 128), BF16),
             pltpu.VMEM((5, 1, 4096), F32),
             pltpu.VMEM((3, 1, 4096), F32),
             pltpu.VMEM((NX, 1, 4096), F32),
             pltpu.VMEM((NZ, 1, 4096), F32),
-            pltpu.SemaphoreType.DMA((2, 2, NC, 5)),
+            pltpu.SemaphoreType.DMA((2, 2, NC, HOPS)),
             pltpu.SemaphoreType.DMA((2, 13)),
             pltpu.SemaphoreType.DMA((2, 10)),
             pltpu.SemaphoreType.DMA((2, 20)),
             pltpu.SemaphoreType.DMA((2, 13)),
+            pltpu.SemaphoreType.DMA((3,)),
         ],
         compiler_params=pltpu.CompilerParams(
             collective_id=0, has_side_effects=True, vmem_limit_bytes=58 * 1024 * 1024
@@ -608,14 +704,33 @@
         lengths,
         target,
         patches,
-        layer_norm_gain[None],
-        layer_norm_bias[None],
+        layer_norm_gain,
+        layer_norm_bias,
         w_qkv,
-        qkv_bias[None],
-        out_grad,
+        qkv_bias,
+        out_grad.T,
     )
+    out = pl.pallas_call(
+        finish,
+        out_shape=(
+            shape((WIDTH, rows), BF16),
+            shape((rows, depth), BF16),
+            shape(w_qkv.shape, F32),
+            shape((depth,), F32),
+            shape((depth,), F32),
+            shape((cols,), F32),
+        ),
+        in_specs=[hbm, hbm, vmem, vmem],
+        out_specs=[hbm, hbm, vmem, vmem, vmem, vmem],
+        scratch_shapes=[
+            pltpu.VMEM((WIDTH, rows), BF16),
+            pltpu.VMEM((rows, depth), BF16),
+            pltpu.SemaphoreType.DMA((3,)),
+            pltpu.SemaphoreType.DMA((3,)),
+        ],
+    )(*parts)
     attn_out, patch_gradient, weight_grad, gain, bias, qbias = out
-    return attn_out, patch_gradient, weight_grad, gain[0], bias[0], qbias[0]
+    return attn_out.T, patch_gradient, weight_grad, gain, bias, qbias
 
 
 def solution(mesh):

time: 141 us -> 109 us (0.77)
  Pallas kernels: 128 us -> 108 us
  local copies, waits for them, and re-layouts: 10.9 us -> 0 us
  other arithmetic: 1.86 us -> 0 us
    pallas_call x1 -> x2, Pallas kernels: 128 us -> 108 us  [the longest x1 104 us: body(): pl.pallas_call(kernel, out_shape=(shape((WIDTH, rows), BF16), shape((rows...]
    unnamed x14 -> x0, local copies, waits for them, and re-layouts: 6.99 us -> none
    broadcast_in_dim x3 -> x0, local copies, waits for them, and re-layouts: 3.88 us -> none  [the longest x1 1.29 us: body(): qkv_bias[None]]
    pallas_call x3 -> x0, other arithmetic: 1.86 us -> none  [body(): pl.pallas_call(kernel, out_shape=(shape((rows, WIDTH), BF16), shape((rows...]
where the time goes in v2:
time: 109 us
  Pallas kernels  108 us (99%)
    pallas_call x1, Pallas kernels, body(): pl.pallas_call(kernel, out_shape=(shape((WIDTH, rows), BF16), shape((rows...  104 us
    pallas_call x1, Pallas kernels, body(): pl.pallas_call(finish, out_shape=(shape((WIDTH, rows), BF16), shape((rows...  4.33 us

profile of v2, /device:TPU:8, one launch (start us, length us, event | category | flops | bytes accessed | tf_op | source)
XLA Modules:
  0.0 108.9 jit_solution(17194566589904253514)
XLA Ops:
  0.6 103.7 %shard_map.127 = (bf16[576,512]{1,0:T(8,128)(2,1)}, bf16[512,1152]{1,0:T(8,128)(2,1)}, bf16[2048,128]{1,0:T(8,128)(2,1)}, f32[1,4096]{1,0:T(1,128)}) custom-call(s32[2]{0:T(128)} %len_ref.1, s32[2]{0:T(128)} %tgt_ref.1, bf16[512,1152]{1,0:T(8,128)(2,1)} %x_hbm.1, f32[1152]{0:T(1024)} %g_ref.1, f32[1152]{0:T(1024)} %b_ref.1, bf16[144,1728]{1,0:T(8,128)(2,1)} %w_hbm.1, ...), custom_call_target="tpu_custom_call" | custom-call | tf_op jit(solution)/shard_map/pallas_call | solution.py:647
  104.4 4.3 %shard_map.128 = (bf16[576,512]{1,0:T(8,128)(2,1)}, bf16[512,1152]{1,0:T(8,128)(2,1)}, f32[144,1728]{1,0:T(8,128)}, f32[1152]{0:T(1024)}, f32[1152]{0:T(1024)}, /*index=5*/f32[1728]{0:T(1024)}) custom-call(bf16[576,512]{1,0:T(8,128)(2,1)} %get-tuple-element.16.ao_in, bf16[512,1152]{1,0:T(8,128)(2,1)} %get-tuple-element.17.pg_in, ...), custom_call_target="tpu_custom_call" | custom-call | tf_op jit(solution)/shard_map/pallas_call | solution.py:713

commit v3 on v2

--- a/solution.py
+++ b/solution.py
@@ -45,6 +45,9 @@
 HOPS = 6
 NC = len(ROUTE)
 HALF_A = 80
+PIECES = 4
+PIECE = 2048 // PIECES
+HALF, QUARTER, SHARE = PIECE // 2, PIECE // NX, PIECE // NX // NZ
 
 
 def window(head):
@@ -355,97 +358,118 @@
         for n, value in gv.items():
             dqkv[rows, 2 * WIDTH + n : 2 * WIDTH + n + value.shape[1]] = value
 
-    def weight_block(owner):
-        return nn(nrmt[pl.ds(pl.multiple_of(owner * 144, 16), 144), :], dqkv[...])
-
-    def put_block(par, j, value, extra):
-        for t in range(14):
-            piece = value[:, t * 128 : min(t * 128 + 128, 3 * WIDTH)]
-            wide = piece.shape[1]
-            if extra is not None:
-                piece = piece + extra[j, pl.ds(t * 144, 144), 0:wide].astype(F32)
-            part[par, j, pl.ds(t * 144, 144), 0:wide] = piece.astype(BF16)
-
-    def rs_copy(i, src, dst, where):
-        return remote(src, dst, rs_sem.at[0, i], rs_sem.at[1, i], where)
-
-    def weights_for_sibling():
-        def step(j, _):
-            put_block(1 - c, j, weight_block(j * 2 + 1 - c), None)
-            rs_copy(j, part.at[1 - c, j], rc.at[j], sib).start()
-            return 0
-
-        lax.fori_loop(0, NY, step, 0)
-
-    def weights_own(order):
-        out = {}
-        for i, j in enumerate(order):
-            rs_copy(j, part.at[1 - c, j], rc.at[j], sib).wait_recv()
-            put_block(c, j, weight_block(j * 2 + c), rc)
-            low, high = part.at[c, j, pl.ds(0, 1024), :], part.at[c, j, pl.ds(1024, 1024), :]
-            if i == 0:
-                out["a0"] = start(rs_copy(4, low, a1.at[0], at_y1))
-                out["b0"] = start(rs_copy(5, high, b1.at[0], at_y3))
-            elif i == 1:
-                out["a1"] = start(rs_copy(6, low, a1.at[1], at_y1))
-            elif i == 2:
-                out["b1"] = start(rs_copy(7, high, b1.at[1], at_y3))
-        return out
+    def weight_tiles(first, last):
+        def step(pair, carry):
+            cols = pl.ds(pl.multiple_of(pair * 256, 256), 256)
+            value = nn(nrmt[...], dqkv[:, cols]).astype(BF16)
+            for owner in range(8):
+                for u in range(2):
+                    row = pl.multiple_of(pair * 288 + u * 144, 16)
+                    part[owner % 2, owner // 2, pl.ds(row, 144), :] = value[
+                        owner * 144 : owner * 144 + 144, u * 128 : u * 128 + 128
+                    ]
+            return carry
+
+        lax.fori_loop(first, last, step, 0)
+
+    def rs_copy(p, i, src, dst, where):
+        return start(remote(src, dst, rs_sem.at[0, p, i], rs_sem.at[1, p, i], where))
+
+    def to_sibling(p):
+        rows = pl.ds(p * PIECE, PIECE)
+        return rs_copy(p, 0, part.at[1 - c, :, rows, :], rc.at[:, rows, :], sib)
 
     def add(*terms):
         total = terms[0].astype(F32)
         for term in terms[1:]:
             total = total + term.astype(F32)
-        return total
-
-    def reduce_second(copies):
+        return total.astype(BF16)
+
+    def reduce_first(p, core):
+        core.wait_recv()
+        rows, half = pl.ds(p * PIECE, PIECE), pl.ds(p * HALF, HALF)
+        low, high = pl.ds(p * PIECE, HALF), pl.ds(p * PIECE + HALF, HALF)
+        out = {}
+        for i, j in enumerate((y2, y1, y3, y)):
+            part[c, j, rows, :] = add(part[c, j, rows, :], rc[j, rows, :])
+            if i == 0:
+                out["a0"] = rs_copy(p, 1, part.at[c, j, low, :], a1.at[0, half, :], at_y1)
+                out["b0"] = rs_copy(p, 2, part.at[c, j, high, :], b1.at[0, half, :], at_y3)
+            elif i == 1:
+                out["a1"] = rs_copy(p, 3, part.at[c, j, low, :], a1.at[1, half, :], at_y1)
+            elif i == 2:
+                out["b1"] = rs_copy(p, 4, part.at[c, j, high, :], b1.at[1, half, :], at_y3)
+        return out
+
+    def reduce_second(p, copies):
+        half = pl.ds(p * HALF, HALF)
+        low, high = pl.ds(p * PIECE, HALF), pl.ds(p * PIECE + HALF, HALF)
         copies["a0"].wait_recv()
-        ta[...] = add(part[c, y3, pl.ds(0, 1024), :], a1[0]).astype(BF16)
-        copies["a2"] = start(rs_copy(8, ta, a2, at_y3))
+        ta[half, :] = add(part[c, y3, low, :], a1[0, half, :])
+        copies["a2"] = rs_copy(p, 5, ta.at[half, :], a2.at[half, :], at_y3)
         copies["b0"].wait_recv()
-        tb[...] = add(part[c, y1, pl.ds(1024, 1024), :], b1[0]).astype(BF16)
-        copies["b2"] = start(rs_copy(9, tb, b2, at_y1))
-
-    def reduce_last(copies):
-        copies["a1"].wait_recv()
-        copies["a2"].wait_recv()
-        gsum[pl.ds(0, 1024), :] = add(part[c, y, pl.ds(0, 1024), :], a1[1], a2[...]).astype(BF16)
-        copies["b1"].wait_recv()
-        copies["b2"].wait_recv()
-        gsum[pl.ds(1024, 1024), :] = add(part[c, y, pl.ds(1024, 1024), :], b1[1], b2[...]).astype(
-            BF16
-        )
-
-    def ar_copy(i, src, dst, where):
-        return start(remote(src, dst, ar_sem.at[0, i], ar_sem.at[1, i], where))
-
-    def ar_x_send():
+        tb[half, :] = add(part[c, y1, high, :], b1[0, half, :])
+        copies["b2"] = rs_copy(p, 6, tb.at[half, :], b2.at[half, :], at_y1)
+
+    def ar_copy(p, i, src, dst, where):
+        return start(remote(src, dst, ar_sem.at[0, p, i], ar_sem.at[1, p, i], where))
+
+    def wait_all(copies):
+        for copy in copies:
+            copy.wait_recv()
+
+    def ar_x_send(p, copies):
+        half = pl.ds(p * HALF, HALF)
+        low, high = pl.ds(p * PIECE, HALF), pl.ds(p * PIECE + HALF, HALF)
+        wait_all([copies["a1"], copies["a2"]])
+        gsum[low, :] = add(part[c, y, low, :], a1[1, half, :], a2[half, :])
+        wait_all([copies["b1"], copies["b2"]])
+        gsum[high, :] = add(part[c, y, high, :], b1[1, half, :], b2[half, :])
         return [
-            ar_copy(j - 1, gsum.at[pl.ds((x + j) % NX * 512, 512), :], rx.at[j - 1], at_x[j])
+            ar_copy(
+                p,
+                j - 1,
+                gsum.at[pl.ds(p * PIECE + (x + j) % NX * QUARTER, QUARTER), :],
+                rx.at[j - 1, pl.ds(p * QUARTER, QUARTER), :],
+                at_x[j],
+            )
             for j in range(1, NX)
         ]
 
-    def ar_z_send(copies):
-        for copy in copies:
-            copy.wait_recv()
-        xs[...] = add(gsum[pl.ds(x * 512, 512), :], rx[0], rx[1], rx[2]).astype(BF16)
+    def ar_z_send(p, copies):
+        wait_all(copies)
+        here = pl.ds(p * QUARTER, QUARTER)
+        xs[here, :] = add(
+            gsum[pl.ds(p * PIECE + x * QUARTER, QUARTER), :], *[rx[j, here, :] for j in range(3)]
+        )
         return [
-            ar_copy(2 + j, xs.at[pl.ds((z + j) % NZ * 64, 64), :], rz.at[j - 1], at_z[j])
+            ar_copy(
+                p,
+                2 + j,
+                xs.at[pl.ds(p * QUARTER + (z + j) % NZ * SHARE, SHARE), :],
+                rz.at[j - 1, pl.ds(p * SHARE, SHARE), :],
+                at_z[j],
+            )
             for j in range(1, NZ)
         ]
 
-    def ar_z_gather(copies):
-        for copy in copies:
-            copy.wait_recv()
-        here = pl.ds(x * 512 + z * 64, 64)
-        full[here, :] = add(xs[pl.ds(z * 64, 64), :], *[rz[j] for j in range(7)]).astype(BF16)
-        return [ar_copy(9 + j, full.at[here, :], full.at[here, :], at_z[j]) for j in range(1, NZ)]
-
-    def ar_x_gather(copies):
-        for copy in copies:
-            copy.wait_recv()
-        here = pl.ds(x * 512, 512)
-        return [ar_copy(16 + j, full.at[here, :], full.at[here, :], at_x[j]) for j in range(1, NX)]
+    def ar_z_gather(p, copies):
+        wait_all(copies)
+        here = pl.ds(p * PIECE + x * QUARTER + z * SHARE, SHARE)
+        full[here, :] = add(
+            xs[pl.ds(p * QUARTER + z * SHARE, SHARE), :],
+            *[rz[j, pl.ds(p * SHARE, SHARE), :] for j in range(7)],
+        )
+        return [
+            ar_copy(p, 9 + j, full.at[here, :], full.at[here, :], at_z[j]) for j in range(1, NZ)
+        ]
+
+    def ar_x_gather(p, copies):
+        wait_all(copies)
+        here = pl.ds(p * PIECE + x * QUARTER, QUARTER)
+        return [
+            ar_copy(p, 16 + j, full.at[here, :], full.at[here, :], at_x[j]) for j in range(1, NX)
+        ]
 
     def v_copy(i, src, dst, where):
         return start(remote(src, dst, v_sem.at[0, i], v_sem.at[1, i], where))
@@ -477,23 +501,19 @@
             total = total + vz[j]
         sums_ref[...] = total
 
-    def input_gradient():
-        def step(i, carry):
-            rows = pl.ds(pl.multiple_of(i * SLOT, SLOT), SLOT)
-            probs_rows = nt(dqkv[rows, :], wf[...]).astype(BF16)
-            nrm[rows, :] = probs_rows
-            return carry
-
-        lax.fori_loop(0, 2, step, 0)
-
+    def norm_gradient(slot):
+        rows = slice(slot * SLOT, slot * SLOT + SLOT)
+        nrm[rows, :] = nt(dqkv[rows, 0 : 3 * WIDTH], wf[...]).astype(BF16)
+
+    def input_gradient(slot):
         def piece(i, carry):
             gsum_, bsum_, qsum_ = carry
-            rows = pl.ds(pl.multiple_of(i * 32, 32), 32)
+            rows = pl.ds(pl.multiple_of(slot * SLOT + i * 32, 32), 32)
             dn = nrm[rows, :].astype(F32)
             h = xh[rows, :]
             gsum_ = gsum_ + jnp.sum(dn * h, axis=0, keepdims=True)
             bsum_ = bsum_ + jnp.sum(dn, axis=0, keepdims=True)
-            qsum_ = qsum_ + jnp.sum(dqkv[rows, :].astype(F32), axis=0, keepdims=True)
+            qsum_ = qsum_ + jnp.sum(dqkv[rows, 0 : 3 * WIDTH].astype(F32), axis=0, keepdims=True)
             d = dn * g_ref[...].reshape(1, -1)
             m1 = jnp.mean(d, axis=-1, keepdims=True)
             m2 = jnp.mean(d * h, axis=-1, keepdims=True)
@@ -501,11 +521,12 @@
             return gsum_, bsum_, qsum_
 
         zero = (jnp.zeros((1, 1152), F32), jnp.zeros((1, 1152), F32), jnp.zeros((1, 1728), F32))
-        gsum_, bsum_, qsum_ = lax.fori_loop(0, 16, piece, zero)
-        vs[0, :, 0:1152] = gsum_
-        vs[0, :, 1152:2304] = bsum_
-        vs[0, :, 2304:4032] = qsum_
-        vs[0, :, 4032:4096] = jnp.zeros((1, 64), F32)
+        sums = lax.fori_loop(0, 8, piece, zero)
+        for first, value in zip((0, 1152, 2304), sums):
+            cols = slice(first, first + value.shape[1])
+            vs[0, :, cols] = value if slot == 0 else vs[0, :, cols] + value
+        if slot == 0:
+            vs[0, :, 4032:4096] = jnp.zeros((1, 64), F32)
 
     def go(advance, slot, k):
         for i in range(NC // 2):
@@ -526,7 +547,7 @@
     for par in range(2):
         for j in range(NY):
             part[par, j, pl.ds(2016, 32), :] = jnp.zeros((32, 128), BF16)
-            part[par, j, pl.ds(13 * 144, 144), :] = jnp.zeros((144, 128), BF16)
+    dqkv[:, 3 * WIDTH :] = jnp.zeros((2 * SLOT, 64), BF16)
     load_x.wait()
     norm(0)
     norm(1)
@@ -556,46 +577,80 @@
     go(advance1, 1, 5)
     backward(0, spread(steps(advance2, 0, 0)))
     backward(1, spread(steps(advance2, 1, 0)))
-    weights_for_sibling()
-    go(advance2, 0, 1)
-    go(advance2, 1, 1)
-    copies = weights_own((y2, y1, y3, y))
-    go(advance2, 0, 2)
-    go(advance2, 1, 2)
-    input_gradient()
-    store_pg = pltpu.make_async_copy(pg_ref, pg_hbm, io_sem.at[0])
-    store_pg.start()
-    va = v_pair(0, sib)
-    go(advance2, 0, 3)
-    v_next(0, va)
-    va = v_pair(1, at_y1)
-    go(advance2, 1, 3)
-    reduce_second(copies)
-    v_next(1, va)
-    va = v_pair(2, at_y3)
-    go(advance2, 0, 4)
-    go(advance2, 1, 4)
-    reduce_last(copies)
-    ar = ar_x_send()
-    v_next(2, va)
-    vc = v_x_send()
+    core, moving = [], {}
+    for p, (first, last) in enumerate(((0, 2), (2, 4), (4, 6), (6, 7))):
+        weight_tiles(first, last)
+        core.append(to_sibling(p))
+        if p == 1:
+            go(advance2, 0, 1)
     store_ao = []
-    for slot in range(2):
+
+    def stage(s, p):
+        if s == 1:
+            moving[p] = reduce_first(p, core[p])
+        elif s == 2:
+            reduce_second(p, moving[p])
+        else:
+            moving[p] = (ar_x_send, ar_z_send, ar_z_gather, ar_x_gather)[s - 3](p, moving[p])
+
+    def store(slot):
         go(advance2, slot, 5)
         copy = pltpu.make_async_copy(
             ao_ref.at[slot], ao_hbm.at[:, pl.ds(slot * SLOT, SLOT)], io_sem.at[1 + slot]
         )
         copy.start()
         store_ao.append(copy)
-    ar = ar_z_send(ar)
+
+    stage(1, 0)
+    stage(1, 1)
+    go(advance2, 1, 1)
+    norm_gradient(0)
+    go(advance2, 0, 2)
+    stage(2, 0)
+    stage(1, 2)
+    go(advance2, 1, 2)
+    input_gradient(0)
+    stage(2, 1)
+    stage(1, 3)
+    go(advance2, 0, 3)
+    stage(3, 0)
+    norm_gradient(1)
+    go(advance2, 1, 3)
+    stage(2, 2)
+    stage(3, 1)
+    stage(4, 0)
+    go(advance2, 0, 4)
+    input_gradient(1)
+    store_pg = pltpu.make_async_copy(pg_ref, pg_hbm, io_sem.at[0])
+    store_pg.start()
+    va = v_pair(0, sib)
+    stage(2, 3)
+    stage(3, 2)
+    go(advance2, 1, 4)
+    stage(4, 1)
+    stage(5, 0)
+    v_next(0, va)
+    va = v_pair(1, at_y1)
+    store(0)
+    stage(3, 3)
+    stage(4, 2)
+    stage(5, 1)
+    stage(6, 0)
+    store(1)
+    v_next(1, va)
+    va = v_pair(2, at_y3)
+    stage(4, 3)
+    stage(5, 2)
+    stage(6, 1)
+    v_next(2, va)
+    vc = v_x_send()
+    stage(5, 3)
+    stage(6, 2)
     vc = v_z_send(vc)
-    ar = ar_z_gather(ar)
-    ar = ar_x_gather(ar)
+    stage(6, 3)
     v_last(vc)
-    for copy in ar:
-        copy.wait_recv()
-    for j in range(NY):
-        rs_copy(j, part.at[1 - c, j], rc.at[j], sib).wait_send()
+    for p in range(PIECES):
+        wait_all(moving[p])
     for copy in pending:
         copy.wait_send()
     store_pg.wait()
@@ -668,7 +723,7 @@
             pltpu.VMEM((rows, WIDTH), BF16),
             pltpu.VMEM((2 * HEADS, SLOT, SLOT), F32),
             pltpu.VMEM((2, WIDTH, SLOT), BF16),
-            pltpu.VMEM((rows, cols), BF16),
+            pltpu.VMEM((rows, cols + 64), BF16),
             pltpu.VMEM((2, WIDTH, SLOT), BF16),
             pltpu.VMEM((5, 2, WIDTH, SLOT), BF16),
             pltpu.VMEM((6, 2, WIDTH, SLOT), BF16),
@@ -692,8 +747,8 @@
             pltpu.VMEM((NZ, 1, 4096), F32),
             pltpu.SemaphoreType.DMA((2, 2, NC, HOPS)),
             pltpu.SemaphoreType.DMA((2, 13)),
-            pltpu.SemaphoreType.DMA((2, 10)),
-            pltpu.SemaphoreType.DMA((2, 20)),
+            pltpu.SemaphoreType.DMA((2, PIECES, 7)),
+            pltpu.SemaphoreType.DMA((2, PIECES, 20)),
             pltpu.SemaphoreType.DMA((2, 13)),
             pltpu.SemaphoreType.DMA((3,)),
         ],

time: 109 us -> 104 us (0.954)
  Pallas kernels: 108 us -> 103 us
    pallas_call x1, Pallas kernels: 104 us -> 98.3 us  [body(): pl.pallas_call(kernel, out_shape=(shape((WIDTH, rows), BF16), shape((rows...]
where the time goes in v3:
time: 104 us; the launch traced here: 103 us
  Pallas kernels  103 us (99%)
    pallas_call x1, Pallas kernels, body(): pl.pallas_call(kernel, out_shape=(shape((WIDTH, rows), BF16), shape((rows...  98.3 us
    pallas_call x1, Pallas kernels, body(): pl.pallas_call(finish, out_shape=(shape((WIDTH, rows), BF16), shape((rows...  4.33 us

profile of v3, /device:TPU:8, one launch (start us, length us, event | category | flops | bytes accessed | tf_op | source)
XLA Modules:
  0.0 103.4 jit_solution(2368078303304270651)
XLA Ops:
  0.6 98.3 %shard_map.127 = (bf16[576,512]{1,0:T(8,128)(2,1)}, bf16[512,1152]{1,0:T(8,128)(2,1)}, bf16[2048,128]{1,0:T(8,128)(2,1)}, f32[1,4096]{1,0:T(1,128)}) custom-call(s32[2]{0:T(128)} %len_ref.1, s32[2]{0:T(128)} %tgt_ref.1, bf16[512,1152]{1,0:T(8,128)(2,1)} %x_hbm.1, f32[1152]{0:T(1024)} %g_ref.1, f32[1152]{0:T(1024)} %b_ref.1, bf16[144,1728]{1,0:T(8,128)(2,1)} %w_hbm.1, ...), custom_call_target="tpu_custom_call" | custom-call | tf_op jit(solution)/shard_map/pallas_call | solution.py:702
  98.9 4.3 %shard_map.128 = (bf16[576,512]{1,0:T(8,128)(2,1)}, bf16[512,1152]{1,0:T(8,128)(2,1)}, f32[144,1728]{1,0:T(8,128)}, f32[1152]{0:T(1024)}, f32[1152]{0:T(1024)}, /*index=5*/f32[1728]{0:T(1024)}) custom-call(bf16[576,512]{1,0:T(8,128)(2,1)} %get-tuple-element.16.ao_in, bf16[512,1152]{1,0:T(8,128)(2,1)} %get-tuple-element.17.pg_in, ...), custom_call_target="tpu_custom_call" | custom-call | tf_op jit(solution)/shard_map/pallas_call | solution.py:768

commit v4 on v3

--- a/solution.py
+++ b/solution.py
@@ -170,6 +170,11 @@
         pending.append(copy)
         return copy
 
+    def drain(count):
+        for copy in pending[:count]:
+            copy.wait_send()
+        del pending[:count]
+
     flip = []
     for slot in range(2):
         mask = jnp.bitwise_xor(tgt_ref[slot], dp)
@@ -568,15 +573,15 @@
     go(advance1, 1, 4)
     project(1)
     forward(0, spread([]))
+    go(advance1, 0, 5)
     for i in range(NC // 2):
         send2(i, 0)
-    go(advance1, 0, 5)
     forward(1, spread([]))
     for i in range(NC // 2):
         send2(NC // 2 + i, 0)
-    go(advance1, 1, 5)
-    backward(0, spread(steps(advance2, 0, 0)))
+    backward(0, spread(steps(advance1, 1, 5) + steps(advance2, 0, 0)))
     backward(1, spread(steps(advance2, 1, 0)))
+    early = len(pending)
     core, moving = [], {}
     for p, (first, last) in enumerate(((0, 2), (2, 4), (4, 6), (6, 7))):
         weight_tiles(first, last)
@@ -629,8 +634,10 @@
     go(advance2, 1, 4)
     stage(4, 1)
     stage(5, 0)
+    drain(early)
     v_next(0, va)
     va = v_pair(1, at_y1)
+    middle = len(pending)
     store(0)
     stage(3, 3)
     stage(4, 2)
@@ -644,24 +651,43 @@
     stage(6, 1)
     v_next(2, va)
     vc = v_x_send()
+    drain(middle)
     stage(5, 3)
     stage(6, 2)
     vc = v_z_send(vc)
+    late = len(pending)
     stage(6, 3)
     v_last(vc)
-    for p in range(PIECES):
-        wait_all(moving[p])
-    for copy in pending:
-        copy.wait_send()
+    drain(late)
     store_pg.wait()
     for copy in store_ao:
         copy.wait()
+    for p in range(PIECES):
+        wait_all(moving[p])
+    drain(len(pending))
 
 
 def finish(
-    ao_in, pg_in, full, sums, ao_out, pg_out, wg_ref, gg_ref, bg_ref, qg_ref, ao, pg, in_sem, out_sem
+    ao_in,
+    pg_in,
+    full_in,
+    sums,
+    ao_out,
+    pg_out,
+    wg_out,
+    gg_ref,
+    bg_ref,
+    qg_ref,
+    ao,
+    pg,
+    full,
+    wg,
+    in_sem,
+    out_sem,
 ):
     half = pg_in.shape[0] // 2
+    part = wg.shape[0] // 3
+    load_full = pltpu.make_async_copy(full_in, full, in_sem.at[3])
     pieces = [
         (ref_in.at[rows, :], ref.at[rows, :], ref_out.at[rows, :])
         for ref_in, ref, ref_out, rows in (
@@ -676,14 +702,22 @@
     stores = [
         pltpu.make_async_copy(mid, dst, out_sem.at[i]) for i, (_, mid, dst) in enumerate(pieces)
     ]
+    load_full.start()
     for load in loads:
         load.start()
-    for load, store in zip(loads, stores):
-        load.wait()
+    load_full.wait()
+    for i in range(3):
+        for t in range(14):
+            wide = min(128, 3 * WIDTH - t * 128)
+            wg[i * part : (i + 1) * part, t * 128 : t * 128 + wide] = full[
+                pl.ds(t * 144 + i * part, part), 0:wide
+            ].astype(F32)
+        rows = pl.ds(i * part, part)
+        store = pltpu.make_async_copy(wg.at[rows, :], wg_out.at[rows, :], out_sem.at[3 + i])
         store.start()
-    for t in range(14):
-        wide = min(128, 3 * WIDTH - t * 128)
-        wg_ref[:, t * 128 : t * 128 + wide] = full[pl.ds(t * 144, 144), 0:wide].astype(F32)
+        stores.append(store)
+        loads[i].wait()
+        stores[i].start()
     gg_ref[...] = sums[0, 0:1152]
     bg_ref[...] = sums[0, 1152:2304]
     qg_ref[...] = sums[0, 2304:4032]
@@ -775,13 +809,15 @@
             shape((depth,), F32),
             shape((cols,), F32),
         ),
-        in_specs=[hbm, hbm, vmem, vmem],
-        out_specs=[hbm, hbm, vmem, vmem, vmem, vmem],
+        in_specs=[hbm, hbm, hbm, vmem],
+        out_specs=[hbm, hbm, hbm, vmem, vmem, vmem],
         scratch_shapes=[
             pltpu.VMEM((WIDTH, rows), BF16),
             pltpu.VMEM((rows, depth), BF16),
-            pltpu.SemaphoreType.DMA((3,)),
-            pltpu.SemaphoreType.DMA((3,)),
+            pltpu.VMEM((2048, 128), BF16),
+            pltpu.VMEM(w_qkv.shape, F32),
+            pltpu.SemaphoreType.DMA((4,)),
+            pltpu.SemaphoreType.DMA((6,)),
         ],
     )(*parts)
     attn_out, patch_gradient, weight_grad, gain, bias, qbias = out

time: 104 us -> 102 us (0.981)
  Pallas kernels: 103 us -> 101 us
    pallas_call x1, Pallas kernels: 98.3 us -> 97.2 us  [body(): pl.pallas_call(kernel, out_shape=(shape((WIDTH, rows), BF16), shape((rows...]
where the time goes in v4:
time: 102 us
  Pallas kernels  101 us (99%)
    pallas_call x1, Pallas kernels, body(): pl.pallas_call(kernel, out_shape=(shape((WIDTH, rows), BF16), shape((rows...  97.2 us
    pallas_call x1, Pallas kernels, body(): pl.pallas_call(finish, out_shape=(shape((WIDTH, rows), BF16), shape((rows...  4.06 us

profile of v4, /device:TPU:8, one launch (start us, length us, event | category | flops | bytes accessed | tf_op | source)
XLA Modules:
  0.0 102.1 jit_solution(16040857689577988070)
XLA Ops:
  0.6 97.2 %shard_map.127 = (bf16[576,512]{1,0:T(8,128)(2,1)}, bf16[512,1152]{1,0:T(8,128)(2,1)}, bf16[2048,128]{1,0:T(8,128)(2,1)}, f32[1,4096]{1,0:T(1,128)}) custom-call(s32[2]{0:T(128)} %len_ref.1, s32[2]{0:T(128)} %tgt_ref.1, bf16[512,1152]{1,0:T(8,128)(2,1)} %x_hbm.1, f32[1152]{0:T(1024)} %g_ref.1, f32[1152]{0:T(1024)} %b_ref.1, bf16[144,1728]{1,0:T(8,128)(2,1)} %w_hbm.1, ...), custom_call_target="tpu_custom_call" | custom-call | tf_op jit(solution)/shard_map/pallas_call | solution.py:736
  97.9 4.1 %shard_map.128 = (bf16[576,512]{1,0:T(8,128)(2,1)}, bf16[512,1152]{1,0:T(8,128)(2,1)}, f32[144,1728]{1,0:T(8,128)}, f32[1152]{0:T(1024)}, f32[1152]{0:T(1024)}, /*index=5*/f32[1728]{0:T(1024)}) custom-call(bf16[576,512]{1,0:T(8,128)(2,1)} %get-tuple-element.16.ao_in, bf16[512,1152]{1,0:T(8,128)(2,1)} %get-tuple-element.17.pg_in, ...), custom_call_target="tpu_custom_call" | custom-call | tf_op jit(solution)/shard_map/pallas_call | solution.py:802

commit v5 on v4

--- a/solution.py
+++ b/solution.py
@@ -42,6 +42,9 @@
 
 
 ROUTE = [(slot, i * CHUNK, CHUNK, chunk_steps(i)) for slot in range(2) for i in range(6)]
+ROUTE2 = [
+    (slot, i * 2 * CHUNK, 2 * CHUNK, chunk_steps(i + 3 * slot)) for slot in range(2) for i in range(3)
+]
 HOPS = 6
 NC = len(ROUTE)
 HALF_A = 80
@@ -192,9 +195,9 @@
                 swap["z", net, stage] = jnp.bitwise_and(jnp.right_shift(word, shift), 1) == 1
         flip.append(swap)
 
-    def route(which, first, sbuf, rbuf, last):
+    def route(which, plan, first, sbuf, rbuf, last):
         def place(ref, i):
-            slot, row, rows, _ = ROUTE[i]
+            slot, row, rows, _ = plan[i]
             if len(ref.shape) == 2:
                 return ref.at[pl.ds(row, rows), pl.ds(slot * SLOT, SLOT)]
             return ref.at[slot, pl.ds(row, rows), :]
@@ -205,7 +208,7 @@
         copies = {}
 
         def send(i, k):
-            order = ROUTE[i][3]
+            order = plan[i][3]
             copies[i, k] = start(
                 remote(
                     source(i, k),
@@ -217,7 +220,7 @@
             )
 
         def advance(i, k):
-            slot, _, _, order = ROUTE[i]
+            slot, _, _, order = plan[i]
             copies[i, k].wait_recv()
             value = jnp.where(
                 flip[slot][order[k]], place(rbuf.at[k], i)[...], source(i, k)[...]
@@ -228,10 +231,11 @@
             else:
                 place(last, i)[...] = value
 
+        advance.half = len(plan) // 2
         return send, advance
 
-    send1, advance1 = route(0, og_ref, s1, r1, do)
-    send2, advance2 = route(1, o, s2, r2, ao_ref)
+    send1, advance1 = route(0, ROUTE, og_ref, s1, r1, do)
+    send2, advance2 = route(1, ROUTE2, o, s2, r2, ao_ref)
 
     def ag(i, src, row, rows, where):
         return start(
@@ -534,8 +538,8 @@
             vs[0, :, 4032:4096] = jnp.zeros((1, 64), F32)
 
     def go(advance, slot, k):
-        for i in range(NC // 2):
-            advance(slot * (NC // 2) + i, k)
+        for i in range(advance.half):
+            advance(slot * advance.half + i, k)
 
     def spread(events):
         events = list(events)
@@ -547,7 +551,7 @@
         return after
 
     def steps(advance, slot, k):
-        return [(advance, slot * (NC // 2) + i, k) for i in range(NC // 2)]
+        return [(advance, slot * advance.half + i, k) for i in range(advance.half)]
 
     for par in range(2):
         for j in range(NY):
@@ -574,11 +578,11 @@
     project(1)
     forward(0, spread([]))
     go(advance1, 0, 5)
-    for i in range(NC // 2):
+    for i in range(3):
         send2(i, 0)
     forward(1, spread([]))
-    for i in range(NC // 2):
-        send2(NC // 2 + i, 0)
+    for i in range(3):
+        send2(3 + i, 0)
     backward(0, spread(steps(advance1, 1, 5) + steps(advance2, 0, 0)))
     backward(1, spread(steps(advance2, 1, 0)))
     early = len(pending)

time: 102 us -> 102 us (level)
  no operation moved by 1% of the time
where the time goes in v5:
time: 102 us
  Pallas kernels  101 us (99%)
    pallas_call x1, Pallas kernels, body(): pl.pallas_call(kernel, out_shape=(shape((WIDTH, rows), BF16), shape((rows...  97 us
    pallas_call x1, Pallas kernels, body(): pl.pallas_call(finish, out_shape=(shape((WIDTH, rows), BF16), shape((rows...  4.06 us

profile of v5, /device:TPU:8, one launch (start us, length us, event | category | flops | bytes accessed | tf_op | source)
XLA Modules:
  0.0 101.8 jit_solution(7512548020770413846)
XLA Ops:
  0.6 97.0 %shard_map.127 = (bf16[576,512]{1,0:T(8,128)(2,1)}, bf16[512,1152]{1,0:T(8,128)(2,1)}, bf16[2048,128]{1,0:T(8,128)(2,1)}, f32[1,4096]{1,0:T(1,128)}) custom-call(s32[2]{0:T(128)} %len_ref.1, s32[2]{0:T(128)} %tgt_ref.1, bf16[512,1152]{1,0:T(8,128)(2,1)} %x_hbm.1, f32[1152]{0:T(1024)} %g_ref.1, f32[1152]{0:T(1024)} %b_ref.1, bf16[144,1728]{1,0:T(8,128)(2,1)} %w_hbm.1, ...), custom_call_target="tpu_custom_call" | custom-call | tf_op jit(solution)/shard_map/pallas_call | solution.py:740
  97.6 4.1 %shard_map.128 = (bf16[576,512]{1,0:T(8,128)(2,1)}, bf16[512,1152]{1,0:T(8,128)(2,1)}, f32[144,1728]{1,0:T(8,128)}, f32[1152]{0:T(1024)}, f32[1152]{0:T(1024)}, /*index=5*/f32[1728]{0:T(1024)}) custom-call(bf16[576,512]{1,0:T(8,128)(2,1)} %get-tuple-element.16.ao_in, bf16[512,1152]{1,0:T(8,128)(2,1)} %get-tuple-element.17.pg_in, ...), custom_call_target="tpu_custom_call" | custom-call | tf_op jit(solution)/shard_map/pallas_call | solution.py:806
